TPU v7x, 512 devices: a whole 4x4x16 slice. The times are simulated.
512 devices in a mesh: inner: 16 (over x_hi, y, core), outer: 32 (over z, x_lo).
Axes of the slice: x: 4 (x_hi: 2, x_lo: 2; x = x_hi * 2 + x_lo), y: 4, z: 16, core: 2. Of those that a mesh axis runs over, the one named last changes fastest.
Arguments:
- query: bfloat16 [65536, 4096], P(('inner', 'outer')), may hold values from -6 to 6
- key: bfloat16 [65536, 512], P(('inner', 'outer')), may hold values from -6 to 6
- value: bfloat16 [65536, 512], P(('inner', 'outer')), may hold values from -6 to 6
- out: bfloat16 [65536, 4096], P(('inner', 'outer')), may hold values from -6 to 6
- dout: bfloat16 [65536, 4096], P(('inner', 'outer')), may hold values from -6 to 6
- lse: float32 [32, 65536], P(None, ('inner', 'outer')), may hold values from 6.5 to 8.5
- segment: int32 [65536], P(('inner', 'outer')), may hold values from 0 to 511, never falling along the last dimension, each value on 1 to 256 neighbouring positions
- bitmap: int32 [512], P(('inner', 'outer')), may hold values from 2 to 65535, as said below
Outputs:
- dquery: bfloat16 [65536, 4096], P(('inner', 'outer'))
- dkey: bfloat16 [65536, 512], P(('inner', 'outer'))
- dvalue: bfloat16 [65536, 512], P(('inner', 'outer'))
Inputs may be any that keep to these rules, and one draw needn't show every extreme that they name: `bitmap`: bit 1 of every entry is set: a tile always sees the tile just before it.
All inputs are finite; a program needn't handle non-finite values.
Results may differ from a plain program's by a relative error of at most 0.006.
Values may be sent and summed in bfloat16 or wider, within the bound.
No kernel may reach another device: no remote copies, remote signals or barrier semaphores. Data moves between devices by JAX's collectives and lax.ppermute only.
A program may use at most 128 MiB of HBM per device.

v0:
```python
import jax
import jax.numpy as jnp
from jax import lax
from jax.sharding import PartitionSpec as P

QUERY_HEADS = 32
KEY_VALUE_HEADS = 4
HEAD_SIZE = 128
VISIBLE_TILES = 16


def shifted(array, axis, by):
    devices = lax.axis_size(axis)
    pairs = [(i, i + by) for i in range(devices) if 0 <= i + by < devices]
    return lax.ppermute(array, axis, pairs)


def from_behind(value, axis, steps):
    count = lax.axis_size(axis)
    pairs = [(source, (source + steps) % count) for source in range(count)]
    return lax.ppermute(value, axis, pairs)


def tile_grads(
    query_grouped,
    output_gradient_grouped,
    logsumexp_grouped,
    delta_grouped,
    q_seg,
    key_tile_rows,
    value_tile_rows,
    k_seg,
    on_diag,
):
    tile_rows = query_grouped.shape[0]
    scale = HEAD_SIZE ** (-0.5)
    key_heads = key_tile_rows.reshape(tile_rows, KEY_VALUE_HEADS, HEAD_SIZE)
    value_heads = value_tile_rows.reshape(tile_rows, KEY_VALUE_HEADS, HEAD_SIZE)
    scores = (
        jnp.einsum("qghd,kgd->ghqk", query_grouped, key_heads, preferred_element_type=jnp.float32)
        * scale
    )
    q_pos = jnp.arange(tile_rows, dtype=jnp.int32)
    causal = jnp.where(on_diag, q_pos[None, :] <= q_pos[:, None], True)
    blocked = (
        (q_seg % 2 == 1)[:, None] & (k_seg % 2 == 1)[None, :] & (q_seg[:, None] != k_seg[None, :])
    )
    allowed = causal & jnp.logical_not(blocked)
    prob = jnp.where(
        allowed[None, None], jnp.exp(scores - logsumexp_grouped[..., None]), jnp.float32(0.0)
    )
    prob_half = prob.astype(jnp.bfloat16)
    dvalue = jnp.einsum(
        "ghqk,qghd->kgd", prob_half, output_gradient_grouped, preferred_element_type=jnp.float32
    )
    dprob = jnp.einsum(
        "qghd,kgd->ghqk", output_gradient_grouped, value_heads, preferred_element_type=jnp.float32
    )
    dscore = (prob * (dprob - delta_grouped[..., None])).astype(jnp.bfloat16)
    dquery = (
        jnp.einsum("ghqk,kgd->qghd", dscore, key_heads, preferred_element_type=jnp.float32) * scale
    )
    dkey = (
        jnp.einsum("ghqk,qghd->kgd", dscore, query_grouped, preferred_element_type=jnp.float32)
        * scale
    )
    return (
        dquery.reshape(tile_rows, QUERY_HEADS * HEAD_SIZE),
        dkey.reshape(tile_rows, KEY_VALUE_HEADS * HEAD_SIZE),
        dvalue.reshape(tile_rows, KEY_VALUE_HEADS * HEAD_SIZE),
    )


def shards(query, key, value, out, dout, lse, segment, bitmap):
    tile_rows = query.shape[0]
    group_size = QUERY_HEADS // KEY_VALUE_HEADS
    query_grouped = query.reshape(tile_rows, KEY_VALUE_HEADS, group_size, HEAD_SIZE)
    output_gradient_grouped = dout.reshape(tile_rows, KEY_VALUE_HEADS, group_size, HEAD_SIZE)
    delta_rows = jnp.sum(
        (dout.astype(jnp.float32) * out.astype(jnp.float32)).reshape(
            tile_rows, QUERY_HEADS, HEAD_SIZE
        ),
        axis=-1,
    )
    delta_grouped = delta_rows.T.reshape(KEY_VALUE_HEADS, group_size, tile_rows)
    logsumexp_grouped = lse.reshape(KEY_VALUE_HEADS, group_size, tile_rows)
    place = lax.axis_index(("inner", "outer"))
    word = bitmap[0]

    def visit(offset, key_tile_rows, value_tile_rows, k_seg):
        live = ((jnp.bitwise_and(jnp.right_shift(word, offset), 1) == 1) | (offset == 0)) & (
            place - offset >= 0
        )

        def compute():
            return tile_grads(
                query_grouped,
                output_gradient_grouped,
                logsumexp_grouped,
                delta_grouped,
                segment,
                key_tile_rows,
                value_tile_rows,
                k_seg,
                offset == 0,
            )

        def nothing():
            return (
                jnp.zeros((tile_rows, QUERY_HEADS * HEAD_SIZE), jnp.float32),
                jnp.zeros((tile_rows, KEY_VALUE_HEADS * HEAD_SIZE), jnp.float32),
                jnp.zeros((tile_rows, KEY_VALUE_HEADS * HEAD_SIZE), jnp.float32),
            )

        return lax.cond(live, compute, nothing)

    dq_first, dk_first, dv_first = visit(jnp.int32(0), key, value, segment)

    def turn(offset, state):
        key_tile_rows, value_tile_rows, k_seg, key_gradient_total, value_gradient_total, dq_acc = (
            state
        )
        key_tile_rows, value_tile_rows, k_seg = shifted(
            (key_tile_rows, value_tile_rows, k_seg), ("inner", "outer"), 1
        )
        key_gradient_total, value_gradient_total = from_behind(
            (key_gradient_total, value_gradient_total), ("inner", "outer"), 1
        )
        dq_part, dk_part, dv_part = visit(offset, key_tile_rows, value_tile_rows, k_seg)
        return (
            key_tile_rows,
            value_tile_rows,
            k_seg,
            key_gradient_total + dk_part,
            value_gradient_total + dv_part,
            dq_acc + dq_part,
        )

    state = lax.fori_loop(
        1, VISIBLE_TILES, turn, (key, value, segment, dk_first, dv_first, dq_first)
    )
    dq_total = state[5]
    dk_total, dv_total = (
        from_behind(state[3].astype(jnp.bfloat16), ("inner", "outer"), 1 - VISIBLE_TILES).astype(
            jnp.float32
        ),
        from_behind(state[4].astype(jnp.bfloat16), ("inner", "outer"), 1 - VISIBLE_TILES).astype(
            jnp.float32
        ),
    )
    return (
        dq_total.astype(jnp.bfloat16),
        dk_total.astype(jnp.bfloat16),
        dv_total.astype(jnp.bfloat16),
    )


def solution(mesh):
    placed = (
        P(("inner", "outer"), None),
        P(("inner", "outer"), None),
        P(("inner", "outer"), None),
        P(("inner", "outer"), None),
        P(("inner", "outer"), None),
        P(None, ("inner", "outer")),
        P(("inner", "outer")),
        P(("inner", "outer")),
    )
    return jax.shard_map(
        shards,
        mesh=mesh,
        in_specs=placed,
        out_specs=(
            P(("inner", "outer"), None),
            P(("inner", "outer"), None),
            P(("inner", "outer"), None),
        ),
        check_vma=False,
    )
```

profile of v0, /device:TPU:148, one launch (start us, length us, event | category | flops | bytes accessed | tf_op | source)
XLA Modules:
  0.0 678.8 jit_solution(18271393042043244714)
XLA Ops:
  10.2 9.2 %conditional.2 = (f32[128,4096]{0,1:T(8,128)S(1)}, f32[128,512]{0,1:T(8,128)}, f32[128,512]{0,1:T(8,128)}) conditional(s32[]{:T(128)} %convert_element_type.41, () %tuple.38, (s32[128]{0:T(128)}, bf16[128,512]{1,0:T(8,128)(2,1)S(1)}, bf16[128,4,8,128]{0,3,2,1:T(8,128)(2,1)S(1)}, f32[32,128]{1,0:T(8,128)S(1)}, bf16[128,512]{1,0:T(8,128)(2,1)}, ...), branch_computations={%region_1.0_spmd, %region_2.3_spmd} | conditional | flops 675448320 | bytes 34047312 | solution.py:115
  19.4 593.5 %while.23 = (s32[]{:T(128)}, bf16[128,512]{0,1:T(8,128)(2,1)}, bf16[128,512]{1,0:T(8,128)(2,1)}, s32[128]{0:T(128)}, f32[128,512]{0,1:T(8,128)}, /*index=5*/f32[...) while((s32[]{:T(128)}, bf16[128,512]{0,1:T(8,128)(2,1)}, ...), condition=%wide.region_6.7_spmd, body=%wide.region_3.6_spmd.sunk | while | flops 676121600 | bytes 46930104 | solution.py:139
  44.9 9.3 %conditional.4 = (f32[128,4096]{0,1:T(8,128)}, f32[128,512]{0,1:T(8,128)S(1)}, f32[128,512]{0,1:T(8,128)}) conditional(s32[]{:T(128)} %convert_element_type.56, () %tuple.57, (s32[]{:T(128)}, s32[128]{0:T(128)}, s32[128]{0:T(128)}, bf16[128,512]{0,1:T(8,128)(2,1)S(1)}, bf16[128,4,8,128]{0,3,2,1:T(8,128)(2,1)S(1)}, /*index=5*/f32[32,128]{1,0:T(8,128)S(1)}, ...), branch_computations={%region_4.4_spmd, %region_5.5_spmd} | conditional | flops 675466240 | bytes 17566298 | solution.py:115
  78.8 6.5 collective-permute-done.2
  87.1 9.3 %conditional.4 = (f32[128,4096]{0,1:T(8,128)}, f32[128,512]{0,1:T(8,128)S(1)}, f32[128,512]{0,1:T(8,128)}) conditional(s32[]{:T(128)} %convert_element_type.56, () %tuple.57, (s32[]{:T(128)}, s32[128]{0:T(128)}, s32[128]{0:T(128)}, bf16[128,512]{0,1:T(8,128)(2,1)S(1)}, bf16[128,4,8,128]{0,3,2,1:T(8,128)(2,1)S(1)}, /*index=5*/f32[32,128]{1,0:T(8,128)S(1)}, ...), branch_computations={%region_4.4_spmd, %region_5.5_spmd} | conditional | flops 675466240 | bytes 17566298 | solution.py:115
  112.7 7.4 %collective-permute-start.2 = (s32[128]{0:T(128)}, s32[128]{0:T(128)}, u32[]{:S(2)}, u32[]{:S(2)}) collective-permute-start(s32[128]{0:T(128)} %get-tuple-element.488), channel_id=1, source_target_pairs={{0,1},{1,2},{2,3},{3,4},{4,5},{5,6},{6,7},{7,8},{8,9},{9,10},{10,1... | collective-permute-start | bytes 1544 | tf_op jit(solution)/shard_map/while/body/eval_jaxpr/ppermute | solution.py:15
  146.8 9.9 %collective-permute-start.1 = (bf16[128,512]{1,0:T(8,128)(2,1)}, bf16[128,512]{1,0:T(8,128)(2,1)S(1)}, u32[]{:S(2)}, u32[]{:S(2)}) collective-permute-start(bf16[128,512]{1,0:T(8,128)(2,1)} %get-tuple-element.487), channel_id=1, source_target_pairs={{0,1},{1,2},{2,3},{3,4},{4,5},{5,6},{6,7},{7,8},{8,9},{9,10},{10,1... | collective-permute-start | bytes 393224 | tf_op jit(solution)/shard_map/while/body/eval_jaxpr/ppermute | solution.py:15
  177.2 7.5 %collective-permute-start.3 = (f32[128,512]{0,1:T(8,128)}, f32[128,512]{0,1:T(8,128)}, u32[]{:S(2)}, u32[]{:S(2)}) collective-permute-start(f32[128,512]{0,1:T(8,128)} %get-tuple-element.489), channel_id=1, source_target_pairs={{0,1},{1,2},{2,3},{3,4},{4,5},{5,6},{6,7},{7,8},{8,9},{9,10},{10,1... | collective-permute-start | bytes 786440 | tf_op jit(solution)/shard_map/while/body/eval_jaxpr/ppermute | solution.py:21
  186.6 7.3 %collective-permute-start = (bf16[128,512]{0,1:T(8,128)(2,1)}, bf16[128,512]{0,1:T(8,128)(2,1)S(1)}, u32[]{:S(2)}, u32[]{:S(2)}) collective-permute-start(bf16[128,512]{0,1:T(8,128)(2,1)} %get-tuple-element.486), channel_id=1, source_target_pairs={{0,1},{1,2},{2,3},{3,4},{4,5},{5,6},{6,7},{7,8},{8,9},{9,10},{10,1... | collective-permute-start | bytes 393224 | tf_op jit(solution)/shard_map/while/body/eval_jaxpr/ppermute | solution.py:15
  216.3 9.3 %collective-permute-start.3 = (f32[128,512]{0,1:T(8,128)}, f32[128,512]{0,1:T(8,128)}, u32[]{:S(2)}, u32[]{:S(2)}) collective-permute-start(f32[128,512]{0,1:T(8,128)} %get-tuple-element.489), channel_id=1, source_target_pairs={{0,1},{1,2},{2,3},{3,4},{4,5},{5,6},{6,7},{7,8},{8,9},{9,10},{10,1... | collective-permute-start | bytes 786440 | tf_op jit(solution)/shard_map/while/body/eval_jaxpr/ppermute | solution.py:21
  247.4 9.3 %conditional.4 = (f32[128,4096]{0,1:T(8,128)}, f32[128,512]{0,1:T(8,128)S(1)}, f32[128,512]{0,1:T(8,128)}) conditional(s32[]{:T(128)} %convert_element_type.56, () %tuple.57, (s32[]{:T(128)}, s32[128]{0:T(128)}, s32[128]{0:T(128)}, bf16[128,512]{0,1:T(8,128)(2,1)S(1)}, bf16[128,4,8,128]{0,3,2,1:T(8,128)(2,1)S(1)}, /*index=5*/f32[32,128]{1,0:T(8,128)S(1)}, ...), branch_computations={%region_4.4_spmd, %region_5.5_spmd} | conditional | flops 675466240 | bytes 17566298 | solution.py:115
  283.9 9.3 %conditional.4 = (f32[128,4096]{0,1:T(8,128)}, f32[128,512]{0,1:T(8,128)S(1)}, f32[128,512]{0,1:T(8,128)}) conditional(s32[]{:T(128)} %convert_element_type.56, () %tuple.57, (s32[]{:T(128)}, s32[128]{0:T(128)}, s32[128]{0:T(128)}, bf16[128,512]{0,1:T(8,128)(2,1)S(1)}, bf16[128,4,8,128]{0,3,2,1:T(8,128)(2,1)S(1)}, /*index=5*/f32[32,128]{1,0:T(8,128)S(1)}, ...), branch_computations={%region_4.4_spmd, %region_5.5_spmd} | conditional | flops 675466240 | bytes 17566298 | solution.py:115
  320.6 9.3 %conditional.4 = (f32[128,4096]{0,1:T(8,128)}, f32[128,512]{0,1:T(8,128)S(1)}, f32[128,512]{0,1:T(8,128)}) conditional(s32[]{:T(128)} %convert_element_type.56, () %tuple.57, (s32[]{:T(128)}, s32[128]{0:T(128)}, s32[128]{0:T(128)}, bf16[128,512]{0,1:T(8,128)(2,1)S(1)}, bf16[128,4,8,128]{0,3,2,1:T(8,128)(2,1)S(1)}, /*index=5*/f32[32,128]{1,0:T(8,128)S(1)}, ...), branch_computations={%region_4.4_spmd, %region_5.5_spmd} | conditional | flops 675466240 | bytes 17566298 | solution.py:115
  348.8 7.0 %collective-permute-start.2 = (s32[128]{0:T(128)}, s32[128]{0:T(128)}, u32[]{:S(2)}, u32[]{:S(2)}) collective-permute-start(s32[128]{0:T(128)} %get-tuple-element.488), channel_id=1, source_target_pairs={{0,1},{1,2},{2,3},{3,4},{4,5},{5,6},{6,7},{7,8},{8,9},{9,10},{10,1... | collective-permute-start | bytes 1544 | tf_op jit(solution)/shard_map/while/body/eval_jaxpr/ppermute | solution.py:15
  359.1 9.3 %conditional.4 = (f32[128,4096]{0,1:T(8,128)}, f32[128,512]{0,1:T(8,128)S(1)}, f32[128,512]{0,1:T(8,128)}) conditional(s32[]{:T(128)} %convert_element_type.56, () %tuple.57, (s32[]{:T(128)}, s32[128]{0:T(128)}, s32[128]{0:T(128)}, bf16[128,512]{0,1:T(8,128)(2,1)S(1)}, bf16[128,4,8,128]{0,3,2,1:T(8,128)(2,1)S(1)}, /*index=5*/f32[32,128]{1,0:T(8,128)S(1)}, ...), branch_computations={%region_4.4_spmd, %region_5.5_spmd} | conditional | flops 675466240 | bytes 17566298 | solution.py:115
  396.7 9.3 %conditional.4 = (f32[128,4096]{0,1:T(8,128)}, f32[128,512]{0,1:T(8,128)S(1)}, f32[128,512]{0,1:T(8,128)}) conditional(s32[]{:T(128)} %convert_element_type.56, () %tuple.57, (s32[]{:T(128)}, s32[128]{0:T(128)}, s32[128]{0:T(128)}, bf16[128,512]{0,1:T(8,128)(2,1)S(1)}, bf16[128,4,8,128]{0,3,2,1:T(8,128)(2,1)S(1)}, /*index=5*/f32[32,128]{1,0:T(8,128)S(1)}, ...), branch_computations={%region_4.4_spmd, %region_5.5_spmd} | conditional | flops 675466240 | bytes 17566298 | solution.py:115
  423.6 5.5 collective-permute-start.2
  434.0 9.3 %conditional.4 = (f32[128,4096]{0,1:T(8,128)}, f32[128,512]{0,1:T(8,128)S(1)}, f32[128,512]{0,1:T(8,128)}) conditional(s32[]{:T(128)} %convert_element_type.56, () %tuple.57, (s32[]{:T(128)}, s32[128]{0:T(128)}, s32[128]{0:T(128)}, bf16[128,512]{0,1:T(8,128)(2,1)S(1)}, bf16[128,4,8,128]{0,3,2,1:T(8,128)(2,1)S(1)}, /*index=5*/f32[32,128]{1,0:T(8,128)S(1)}, ...), branch_computations={%region_4.4_spmd, %region_5.5_spmd} | conditional | flops 675466240 | bytes 17566298 | solution.py:115
  464.5 12.3 %collective-permute-start.1 = (bf16[128,512]{1,0:T(8,128)(2,1)}, bf16[128,512]{1,0:T(8,128)(2,1)S(1)}, u32[]{:S(2)}, u32[]{:S(2)}) collective-permute-start(bf16[128,512]{1,0:T(8,128)(2,1)} %get-tuple-element.487), channel_id=1, source_target_pairs={{0,1},{1,2},{2,3},{3,4},{4,5},{5,6},{6,7},{7,8},{8,9},{9,10},{10,1... | collective-permute-start | bytes 393224 | tf_op jit(solution)/shard_map/while/body/eval_jaxpr/ppermute | solution.py:15
  499.1 7.8 %collective-permute-start.4 = (f32[128,512]{0,1:T(8,128)}, f32[128,512]{0,1:T(8,128)}, u32[]{:S(2)}, u32[]{:S(2)}) collective-permute-start(f32[128,512]{0,1:T(8,128)} %get-tuple-element.490), channel_id=1, source_target_pairs={{0,1},{1,2},{2,3},{3,4},{4,5},{5,6},{6,7},{7,8},{8,9},{9,10},{10,1... | collective-permute-start | bytes 786440 | tf_op jit(solution)/shard_map/while/body/eval_jaxpr/ppermute | solution.py:21
  549.3 8.1 %collective-permute-start.2 = (s32[128]{0:T(128)}, s32[128]{0:T(128)}, u32[]{:S(2)}, u32[]{:S(2)}) collective-permute-start(s32[128]{0:T(128)} %get-tuple-element.488), channel_id=1, source_target_pairs={{0,1},{1,2},{2,3},{3,4},{4,5},{5,6},{6,7},{7,8},{8,9},{9,10},{10,1... | collective-permute-start | bytes 1544 | tf_op jit(solution)/shard_map/while/body/eval_jaxpr/ppermute | solution.py:15
  581.7 10.8 %collective-permute-start.1 = (bf16[128,512]{1,0:T(8,128)(2,1)}, bf16[128,512]{1,0:T(8,128)(2,1)S(1)}, u32[]{:S(2)}, u32[]{:S(2)}) collective-permute-start(bf16[128,512]{1,0:T(8,128)(2,1)} %get-tuple-element.487), channel_id=1, source_target_pairs={{0,1},{1,2},{2,3},{3,4},{4,5},{5,6},{6,7},{7,8},{8,9},{9,10},{10,1... | collective-permute-start | bytes 393224 | tf_op jit(solution)/shard_map/while/body/eval_jaxpr/ppermute | solution.py:15
  614.0 21.0 %collective-permute-start.5 = (bf16[128,512]{1,0:T(8,128)(2,1)S(1)}, bf16[128,512]{1,0:T(8,128)(2,1)S(1)}, u32[]{:S(2)}, u32[]{:S(2)}) collective-permute-start(bf16[128,512]{1,0:T(8,128)(2,1)S(1)} %copy.53), channel_id=1, source_target_pairs={{0,497},{1,498},{2,499},{3,500},{4,501},{5,502},{6,503},{7,504},{8... | collective-permute-start | bytes 393224 | tf_op jit(solution)/shard_map/ppermute | solution.py:21
  639.3 36.3 %collective-permute-done.5 = bf16[128,512]{1,0:T(8,128)(2,1)S(1)} collective-permute-done((bf16[128,512]{1,0:T(8,128)(2,1)S(1)}, bf16[128,512]{1,0:T(8,128)(2,1)S(1)}, u32[]{:S(2)}, u32[]{:S(2)}) %collective-permute-start.5) | collective-permute-done | bytes 131104 | tf_op jit(solution)/shard_map/ppermute | solution.py:21
  (510 shorter events, 525.6 us)
Async XLA Ops:
  19.4 39.9 %collective-permute-start.3 = (f32[128,512]{0,1:T(8,128)}, f32[128,512]{0,1:T(8,128)}, u32[]{:S(2)}, u32[]{:S(2)}) collective-permute-start(f32[128,512]{0,1:T(8,128)} %get-tuple-element.489), channel_id=1, source_target_pairs={{0,1},{1,2},{2,3},{3,4},{4,5},{5,6},{6,7},{7,8},{8,9},{9,10},{10,1... | collective-permute-start | bytes 786440 | tf_op jit(solution)/shard_map/while/body/eval_jaxpr/ppermute | solution.py:21
  22.5 38.5 %collective-permute-start.4 = (f32[128,512]{0,1:T(8,128)}, f32[128,512]{0,1:T(8,128)}, u32[]{:S(2)}, u32[]{:S(2)}) collective-permute-start(f32[128,512]{0,1:T(8,128)} %get-tuple-element.490), channel_id=1, source_target_pairs={{0,1},{1,2},{2,3},{3,4},{4,5},{5,6},{6,7},{7,8},{8,9},{9,10},{10,1... | collective-permute-start | bytes 786440 | tf_op jit(solution)/shard_map/while/body/eval_jaxpr/ppermute | solution.py:21
  62.7 38.8 %collective-permute-start.3 = (f32[128,512]{0,1:T(8,128)}, f32[128,512]{0,1:T(8,128)}, u32[]{:S(2)}, u32[]{:S(2)}) collective-permute-start(f32[128,512]{0,1:T(8,128)} %get-tuple-element.489), channel_id=1, source_target_pairs={{0,1},{1,2},{2,3},{3,4},{4,5},{5,6},{6,7},{7,8},{8,9},{9,10},{10,1... | collective-permute-start | bytes 786440 | tf_op jit(solution)/shard_map/while/body/eval_jaxpr/ppermute | solution.py:21
  64.6 38.6 %collective-permute-start.4 = (f32[128,512]{0,1:T(8,128)}, f32[128,512]{0,1:T(8,128)}, u32[]{:S(2)}, u32[]{:S(2)}) collective-permute-start(f32[128,512]{0,1:T(8,128)} %get-tuple-element.490), channel_id=1, source_target_pairs={{0,1},{1,2},{2,3},{3,4},{4,5},{5,6},{6,7},{7,8},{8,9},{9,10},{10,1... | collective-permute-start | bytes 786440 | tf_op jit(solution)/shard_map/while/body/eval_jaxpr/ppermute | solution.py:21
  136.4 37.3 %collective-permute-start.3 = (f32[128,512]{0,1:T(8,128)}, f32[128,512]{0,1:T(8,128)}, u32[]{:S(2)}, u32[]{:S(2)}) collective-permute-start(f32[128,512]{0,1:T(8,128)} %get-tuple-element.489), channel_id=1, source_target_pairs={{0,1},{1,2},{2,3},{3,4},{4,5},{5,6},{6,7},{7,8},{8,9},{9,10},{10,1... | collective-permute-start | bytes 786440 | tf_op jit(solution)/shard_map/while/body/eval_jaxpr/ppermute | solution.py:21
  138.4 37.0 %collective-permute-start.4 = (f32[128,512]{0,1:T(8,128)}, f32[128,512]{0,1:T(8,128)}, u32[]{:S(2)}, u32[]{:S(2)}) collective-permute-start(f32[128,512]{0,1:T(8,128)} %get-tuple-element.490), channel_id=1, source_target_pairs={{0,1},{1,2},{2,3},{3,4},{4,5},{5,6},{6,7},{7,8},{8,9},{9,10},{10,1... | collective-permute-start | bytes 786440 | tf_op jit(solution)/shard_map/while/body/eval_jaxpr/ppermute | solution.py:21
  177.2 35.7 %collective-permute-start.3 = (f32[128,512]{0,1:T(8,128)}, f32[128,512]{0,1:T(8,128)}, u32[]{:S(2)}, u32[]{:S(2)}) collective-permute-start(f32[128,512]{0,1:T(8,128)} %get-tuple-element.489), channel_id=1, source_target_pairs={{0,1},{1,2},{2,3},{3,4},{4,5},{5,6},{6,7},{7,8},{8,9},{9,10},{10,1... | collective-permute-start | bytes 786440 | tf_op jit(solution)/shard_map/while/body/eval_jaxpr/ppermute | solution.py:21
  216.3 45.5 %collective-permute-start.3 = (f32[128,512]{0,1:T(8,128)}, f32[128,512]{0,1:T(8,128)}, u32[]{:S(2)}, u32[]{:S(2)}) collective-permute-start(f32[128,512]{0,1:T(8,128)} %get-tuple-element.489), channel_id=1, source_target_pairs={{0,1},{1,2},{2,3},{3,4},{4,5},{5,6},{6,7},{7,8},{8,9},{9,10},{10,1... | collective-permute-start | bytes 786440 | tf_op jit(solution)/shard_map/while/body/eval_jaxpr/ppermute | solution.py:21
  225.6 38.0 %collective-permute-start.4 = (f32[128,512]{0,1:T(8,128)}, f32[128,512]{0,1:T(8,128)}, u32[]{:S(2)}, u32[]{:S(2)}) collective-permute-start(f32[128,512]{0,1:T(8,128)} %get-tuple-element.490), channel_id=1, source_target_pairs={{0,1},{1,2},{2,3},{3,4},{4,5},{5,6},{6,7},{7,8},{8,9},{9,10},{10,1... | collective-permute-start | bytes 786440 | tf_op jit(solution)/shard_map/while/body/eval_jaxpr/ppermute | solution.py:21
  301.7 33.2 %collective-permute-start.3 = (f32[128,512]{0,1:T(8,128)}, f32[128,512]{0,1:T(8,128)}, u32[]{:S(2)}, u32[]{:S(2)}) collective-permute-start(f32[128,512]{0,1:T(8,128)} %get-tuple-element.489), channel_id=1, source_target_pairs={{0,1},{1,2},{2,3},{3,4},{4,5},{5,6},{6,7},{7,8},{8,9},{9,10},{10,1... | collective-permute-start | bytes 786440 | tf_op jit(solution)/shard_map/while/body/eval_jaxpr/ppermute | solution.py:21
  338.4 35.1 %collective-permute-start.3 = (f32[128,512]{0,1:T(8,128)}, f32[128,512]{0,1:T(8,128)}, u32[]{:S(2)}, u32[]{:S(2)}) collective-permute-start(f32[128,512]{0,1:T(8,128)} %get-tuple-element.489), channel_id=1, source_target_pairs={{0,1},{1,2},{2,3},{3,4},{4,5},{5,6},{6,7},{7,8},{8,9},{9,10},{10,1... | collective-permute-start | bytes 786440 | tf_op jit(solution)/shard_map/while/body/eval_jaxpr/ppermute | solution.py:21
  340.4 34.8 %collective-permute-start.4 = (f32[128,512]{0,1:T(8,128)}, f32[128,512]{0,1:T(8,128)}, u32[]{:S(2)}, u32[]{:S(2)}) collective-permute-start(f32[128,512]{0,1:T(8,128)} %get-tuple-element.490), channel_id=1, source_target_pairs={{0,1},{1,2},{2,3},{3,4},{4,5},{5,6},{6,7},{7,8},{8,9},{9,10},{10,1... | collective-permute-start | bytes 786440 | tf_op jit(solution)/shard_map/while/body/eval_jaxpr/ppermute | solution.py:21
  377.0 34.1 %collective-permute-start.3 = (f32[128,512]{0,1:T(8,128)}, f32[128,512]{0,1:T(8,128)}, u32[]{:S(2)}, u32[]{:S(2)}) collective-permute-start(f32[128,512]{0,1:T(8,128)} %get-tuple-element.489), channel_id=1, source_target_pairs={{0,1},{1,2},{2,3},{3,4},{4,5},{5,6},{6,7},{7,8},{8,9},{9,10},{10,1... | collective-permute-start | bytes 786440 | tf_op jit(solution)/shard_map/while/body/eval_jaxpr/ppermute | solution.py:21
  414.5 33.9 %collective-permute-start.3 = (f32[128,512]{0,1:T(8,128)}, f32[128,512]{0,1:T(8,128)}, u32[]{:S(2)}, u32[]{:S(2)}) collective-permute-start(f32[128,512]{0,1:T(8,128)} %get-tuple-element.489), channel_id=1, source_target_pairs={{0,1},{1,2},{2,3},{3,4},{4,5},{5,6},{6,7},{7,8},{8,9},{9,10},{10,1... | collective-permute-start | bytes 786440 | tf_op jit(solution)/shard_map/while/body/eval_jaxpr/ppermute | solution.py:21
  416.4 33.7 %collective-permute-start.4 = (f32[128,512]{0,1:T(8,128)}, f32[128,512]{0,1:T(8,128)}, u32[]{:S(2)}, u32[]{:S(2)}) collective-permute-start(f32[128,512]{0,1:T(8,128)} %get-tuple-element.490), channel_id=1, source_target_pairs={{0,1},{1,2},{2,3},{3,4},{4,5},{5,6},{6,7},{7,8},{8,9},{9,10},{10,1... | collective-permute-start | bytes 786440 | tf_op jit(solution)/shard_map/while/body/eval_jaxpr/ppermute | solution.py:21
  451.9 41.8 %collective-permute-start.3 = (f32[128,512]{0,1:T(8,128)}, f32[128,512]{0,1:T(8,128)}, u32[]{:S(2)}, u32[]{:S(2)}) collective-permute-start(f32[128,512]{0,1:T(8,128)} %get-tuple-element.489), channel_id=1, source_target_pairs={{0,1},{1,2},{2,3},{3,4},{4,5},{5,6},{6,7},{7,8},{8,9},{9,10},{10,1... | collective-permute-start | bytes 786440 | tf_op jit(solution)/shard_map/while/body/eval_jaxpr/ppermute | solution.py:21
  455.5 39.9 %collective-permute-start.4 = (f32[128,512]{0,1:T(8,128)}, f32[128,512]{0,1:T(8,128)}, u32[]{:S(2)}, u32[]{:S(2)}) collective-permute-start(f32[128,512]{0,1:T(8,128)} %get-tuple-element.490), channel_id=1, source_target_pairs={{0,1},{1,2},{2,3},{3,4},{4,5},{5,6},{6,7},{7,8},{8,9},{9,10},{10,1... | collective-permute-start | bytes 786440 | tf_op jit(solution)/shard_map/while/body/eval_jaxpr/ppermute | solution.py:21
  497.2 34.0 %collective-permute-start.3 = (f32[128,512]{0,1:T(8,128)}, f32[128,512]{0,1:T(8,128)}, u32[]{:S(2)}, u32[]{:S(2)}) collective-permute-start(f32[128,512]{0,1:T(8,128)} %get-tuple-element.489), channel_id=1, source_target_pairs={{0,1},{1,2},{2,3},{3,4},{4,5},{5,6},{6,7},{7,8},{8,9},{9,10},{10,1... | collective-permute-start | bytes 786440 | tf_op jit(solution)/shard_map/while/body/eval_jaxpr/ppermute | solution.py:21
  499.1 33.8 %collective-permute-start.4 = (f32[128,512]{0,1:T(8,128)}, f32[128,512]{0,1:T(8,128)}, u32[]{:S(2)}, u32[]{:S(2)}) collective-permute-start(f32[128,512]{0,1:T(8,128)} %get-tuple-element.490), channel_id=1, source_target_pairs={{0,1},{1,2},{2,3},{3,4},{4,5},{5,6},{6,7},{7,8},{8,9},{9,10},{10,1... | collective-permute-start | bytes 786440 | tf_op jit(solution)/shard_map/while/body/eval_jaxpr/ppermute | solution.py:21
  534.6 33.4 %collective-permute-start.3 = (f32[128,512]{0,1:T(8,128)}, f32[128,512]{0,1:T(8,128)}, u32[]{:S(2)}, u32[]{:S(2)}) collective-permute-start(f32[128,512]{0,1:T(8,128)} %get-tuple-element.489), channel_id=1, source_target_pairs={{0,1},{1,2},{2,3},{3,4},{4,5},{5,6},{6,7},{7,8},{8,9},{9,10},{10,1... | collective-permute-start | bytes 786440 | tf_op jit(solution)/shard_map/while/body/eval_jaxpr/ppermute | solution.py:21
  571.5 38.0 %collective-permute-start.3 = (f32[128,512]{0,1:T(8,128)}, f32[128,512]{0,1:T(8,128)}, u32[]{:S(2)}, u32[]{:S(2)}) collective-permute-start(f32[128,512]{0,1:T(8,128)} %get-tuple-element.489), channel_id=1, source_target_pairs={{0,1},{1,2},{2,3},{3,4},{4,5},{5,6},{6,7},{7,8},{8,9},{9,10},{10,1... | collective-permute-start | bytes 786440 | tf_op jit(solution)/shard_map/while/body/eval_jaxpr/ppermute | solution.py:21
  575.7 35.4 %collective-permute-start.4 = (f32[128,512]{0,1:T(8,128)}, f32[128,512]{0,1:T(8,128)}, u32[]{:S(2)}, u32[]{:S(2)}) collective-permute-start(f32[128,512]{0,1:T(8,128)} %get-tuple-element.490), channel_id=1, source_target_pairs={{0,1},{1,2},{2,3},{3,4},{4,5},{5,6},{6,7},{7,8},{8,9},{9,10},{10,1... | collective-permute-start | bytes 786440 | tf_op jit(solution)/shard_map/while/body/eval_jaxpr/ppermute | solution.py:21
  614.0 61.6 %collective-permute-start.5 = (bf16[128,512]{1,0:T(8,128)(2,1)S(1)}, bf16[128,512]{1,0:T(8,128)(2,1)S(1)}, u32[]{:S(2)}, u32[]{:S(2)}) collective-permute-start(bf16[128,512]{1,0:T(8,128)(2,1)S(1)} %copy.53), channel_id=1, source_target_pairs={{0,497},{1,498},{2,499},{3,500},{4,501},{5,502},{6,503},{7,504},{8... | collective-permute-start | bytes 393224 | tf_op jit(solution)/shard_map/ppermute | solution.py:21
  636.0 41.4 %collective-permute-start.6 = (bf16[128,512]{1,0:T(8,128)(2,1)S(1)}, bf16[128,512]{1,0:T(8,128)(2,1)S(1)}, u32[]{:S(2)}, u32[]{:S(2)}) collective-permute-start(bf16[128,512]{1,0:T(8,128)(2,1)S(1)} %copy.54), channel_id=1, source_target_pairs={{0,497},{1,498},{2,499},{3,500},{4,501},{5,502},{6,503},{7,504},{8... | collective-permute-start | bytes 393224 | tf_op jit(solution)/shard_map/ppermute | solution.py:21
  (135 other events, 1438.2 us)
where the time goes:
time: 685 us; the launch traced here: 679 us
  starting transfers between devices  301 us (44%)
  other arithmetic  123 us (18%)
  waiting for transfers between devices  98.3 us (14%)
  local copies, waits for them, and re-layouts  84.6 us (12%)
  matrix products  60.7 us (9%)
  loops' own time  11.2 us (2%)
    ppermute x45, starting transfers between devices, shifted(): return lax.ppermute(array, axis, pairs)  173 us
    ppermute x32, starting transfers between devices, from_behind(): return lax.ppermute(value, axis, pairs)  128 us
    ppermute x45, waiting for transfers between devices, shifted(): return lax.ppermute(array, axis, pairs)  60.1 us
    add x15, other arithmetic, turn(): dq_acc + dq_part  56.5 us
    while x165, local copies, waits for them, and re-layouts  46.7 us
    ppermute x32, waiting for transfers between devices, from_behind(): return lax.ppermute(value, axis, pairs)  38.2 us
    add x15, other arithmetic, turn(): value_gradient_total + dv_part  26.3 us
    add x15, other arithmetic, turn(): key_gradient_total + dk_part  25.4 us
  transfers between devices with their start and end apart: 77, of which 17 were waited for; matrix products, arithmetic and copies ran while one was open for 31% of the time, Pallas kernels for 0%

commit v1 on v0

v1 whole, which is shorter than its diff:
```python
import functools
import math

import jax
import jax.numpy as jnp
from jax import lax
from jax.experimental import pallas as pl
from jax.experimental.pallas import tpu as pltpu
from jax.sharding import PartitionSpec as P

QUERY_HEADS = 32
KEY_VALUE_HEADS = 4
HEAD_SIZE = 128
VISIBLE_TILES = 16
TILE = 128
GROUP = QUERY_HEADS // KEY_VALUE_HEADS

MY_HEADS = QUERY_HEADS // 2
MY_KV = KEY_VALUE_HEADS // 2
KV_COLS = MY_KV * HEAD_SIZE
Q_COLS = MY_HEADS * HEAD_SIZE
HOPS = VISIBLE_TILES // 2

SEG_ROWS = 16
K1, V1, SEG, K0, V0 = 0, TILE, 2 * TILE, 2 * TILE + SEG_ROWS, 3 * TILE + SEG_ROWS
HALF_ROWS = 2 * TILE + SEG_ROWS
FULL_ROWS = 4 * TILE + SEG_ROWS

SMALL_ROWS = 40
SCALE = HEAD_SIZE**-0.5
LOG2E = math.log2(math.e)
NEVER = -1e30
AXES = ("inner", "outer")


def shift(array, by):
    count = lax.axis_size(AXES)
    pairs = [(i, i + by) for i in range(count) if 0 <= i + by < count]
    return lax.ppermute(array, AXES, pairs)


def swap(array):
    count = lax.axis_size(AXES)
    return lax.ppermute(array, AXES, [(i, i ^ 1) for i in range(count)])


def nt(a, b):
    return lax.dot_general(a, b, (((1,), (1,)), ((), ())), preferred_element_type=jnp.float32)


def nn(a, b):
    return jnp.dot(a, b, preferred_element_type=jnp.float32)


def turn_kernel(column_ref, q_own, do_own, q_par, sm_own, sm_par, q_turned, do_turned, columns):
    column = column_ref[0]

    @pl.loop(0, MY_KV)
    def _(kv):
        first = pl.multiple_of(kv * GROUP, GROUP)
        rows = []
        for at in (first, MY_HEADS + first):
            rows.append(
                jnp.concatenate([sm_own[pl.ds(at, GROUP), :], sm_par[pl.ds(at, GROUP), :]], axis=1)
            )
        rows.append(jnp.zeros((TILE - 2 * GROUP, 2 * TILE), jnp.float32))
        columns[kv] = jnp.concatenate(rows, axis=0).T
        for i in range(GROUP):
            head = first + i
            cols = pl.ds(pl.multiple_of(head * HEAD_SIZE, HEAD_SIZE), HEAD_SIZE)
            own_cols = pl.ds(
                pl.multiple_of((column * MY_HEADS + head) * HEAD_SIZE, HEAD_SIZE), HEAD_SIZE
            )
            at = slice(i * 2 * TILE, (i + 1) * 2 * TILE)
            q_turned[kv, :, at] = jnp.concatenate(
                [q_own[:, own_cols].T, q_par[0:TILE, cols].T], axis=1
            )
            do_turned[kv, :, at] = jnp.concatenate(
                [do_own[:, own_cols].T, q_par[TILE : 2 * TILE, cols].T], axis=1
            )


def turned(column, query, dout, other, sm_own, sm_par):
    here = pl.BlockSpec(memory_space=pltpu.VMEM)
    wide = jax.ShapeDtypeStruct((MY_KV, HEAD_SIZE, GROUP * 2 * TILE), jnp.bfloat16)
    return pl.pallas_call(
        turn_kernel,
        in_specs=[pl.BlockSpec(memory_space=pltpu.SMEM)] + [here] * 5,
        out_specs=[here] * 3,
        out_shape=[wide, wide, jax.ShapeDtypeStruct((MY_KV, 2 * TILE, TILE), jnp.float32)],
        compiler_params=pltpu.CompilerParams(vmem_limit_bytes=16 * 1024 * 1024),
        cost_estimate=pl.CostEstimate(flops=2**20, bytes_accessed=2**23, transcendentals=0),
    )(column[None].astype(jnp.int32), query, dout, other, sm_own, sm_par)


def pair_kernel(offsets, first, last, where_ref, *refs):
    count = len(offsets)
    q_own, q_par, do_own, sm_own, sm_par, q_turned, do_turned, columns = refs[:8]
    blocks = refs[8 : 8 + count]
    at = 8 + count
    dq_in = None
    if not first:
        dq_in = refs[at]
        at += 1
    parts = refs[at : at + count]
    at += count
    if last:
        dq_own, dq_par = refs[at : at + 2]
        at += 2
    else:
        dq_out = refs[at]
        at += 1
    biases = refs[at : at + count]
    column, place = where_ref[0], where_ref[1]

    row = lax.broadcasted_iota(jnp.int32, (TILE, TILE), 0)
    col = lax.broadcasted_iota(jnp.int32, (TILE, TILE), 1)
    for r, small in enumerate((sm_own, sm_par)):
        xq = column if r == 0 else 1 - column
        tile = place - column + xq
        words = small[2 * MY_HEADS + 1 : 2 * MY_HEADS + 2, :].astype(jnp.int32)
        q_seg = jnp.broadcast_to(small[2 * MY_HEADS : 2 * MY_HEADS + 1, :], (TILE, TILE)).T
        for n, s in enumerate(offsets):
            seg = blocks[n][SEG : SEG + SEG_ROWS, :TILE].astype(jnp.float32)
            for t in (1,) if s == HOPS else (0, 1):
                k_seg = jnp.broadcast_to(seg[1 - t : 2 - t, :], (TILE, TILE))
                w = 2 * s + xq - t
                bit = lax.shift_right_logical(words, jnp.broadcast_to(jnp.maximum(w, 0), words.shape)) & 1
                inside = (w >= 0) & (w < VISIBLE_TILES) & (tile - w >= 0)
                bit = jnp.where(w == 0, 1, bit)
                bit = jnp.where(inside, bit, 0)
                seen = (k_seg * q_seg * (k_seg - q_seg) == 0.0) & (
                    jnp.broadcast_to(bit, (TILE, TILE)) == 1
                )
                if s == 0:
                    seen = seen & ((row >= col) | (w != 0))
                k_at = 0 if s == HOPS else t * TILE
                biases[n][r * TILE : (r + 1) * TILE, k_at : k_at + TILE] = jnp.where(
                    seen, 0.0, NEVER
                )

    @pl.loop(0, MY_KV)
    def _(kv):
        kv_cols = pl.ds(pl.multiple_of(kv * HEAD_SIZE, HEAD_SIZE), HEAD_SIZE)
        loaded = []
        for n, s in enumerate(offsets):
            block = blocks[n]
            if s == HOPS:
                k, v = block[K1 : K1 + TILE, kv_cols], block[V1 : V1 + TILE, kv_cols]
            else:
                k = jnp.concatenate(
                    [block[K0 : K0 + TILE, kv_cols], block[K1 : K1 + TILE, kv_cols]], axis=0
                )
                v = jnp.concatenate(
                    [block[V0 : V0 + TILE, kv_cols], block[V1 : V1 + TILE, kv_cols]], axis=0
                )
            loaded.append((k, v, k.T, v.T))
        q_heads, do_heads = [], []
        for i in range(GROUP):
            head = kv * GROUP + i
            cols = pl.ds(pl.multiple_of(head * HEAD_SIZE, HEAD_SIZE), HEAD_SIZE)
            own_cols = pl.ds(
                pl.multiple_of((column * MY_HEADS + head) * HEAD_SIZE, HEAD_SIZE), HEAD_SIZE
            )
            q_heads += [q_own[:, own_cols], q_par[0:TILE, cols]]
            do_heads += [do_own[:, own_cols], q_par[TILE : 2 * TILE, cols]]
        q = jnp.concatenate(q_heads, axis=0)
        do = jnp.concatenate(do_heads, axis=0)
        totals = []
        dq = None
        for n in range(count):
            k, v, k_turned, v_turned = loaded[n]
            scores = nn(q, k_turned)
            dprob = nn(do, v_turned)
            probs, dscores = [], []
            for i in range(GROUP):
                at = slice(i * 2 * TILE, (i + 1) * 2 * TILE)
                neg_lse = columns[kv, :, i : i + 1]
                delta = columns[kv, :, GROUP + i : GROUP + i + 1]
                prob = jnp.exp2(scores[at] * (SCALE * LOG2E) + (biases[n][...] + neg_lse))
                probs.append(prob.astype(jnp.bfloat16))
                dscores.append((prob * (dprob[at] - delta)).astype(jnp.bfloat16))
            prob = jnp.concatenate(probs, axis=0)
            dscore = jnp.concatenate(dscores, axis=0)
            totals.append((nn(q_turned[kv], dscore), nn(do_turned[kv], prob)))
            more = nn(dscore, k)
            dq = more if dq is None else dq + more
        for i in range(GROUP):
            head = kv * GROUP + i
            cols = pl.ds(pl.multiple_of(head * HEAD_SIZE, HEAD_SIZE), HEAD_SIZE)
            part = dq[i * 2 * TILE : (i + 1) * 2 * TILE]
            if not first:
                part = part + dq_in[head]
            if last:
                part = (part * SCALE).astype(jnp.bfloat16)
                dq_own[:, cols] = part[:TILE]
                dq_par[:, cols] = part[TILE:]
            else:
                dq_out[head] = part
        for n, s in enumerate(offsets):
            dk_all = (totals[n][0] * SCALE).T.astype(jnp.bfloat16)
            dv_all = totals[n][1].T.astype(jnp.bfloat16)
            if s == HOPS:
                parts[n][0:TILE, kv_cols] = dk_all
                parts[n][TILE : 2 * TILE, kv_cols] = dv_all
            else:
                parts[n][0:TILE, kv_cols] = dk_all[TILE:]
                parts[n][TILE : 2 * TILE, kv_cols] = dv_all[TILE:]
                parts[n][2 * TILE : 3 * TILE, kv_cols] = dk_all[:TILE]
                parts[n][3 * TILE : 4 * TILE, kv_cols] = dv_all[:TILE]


def pair_grads(offsets, where, query, dout, other, sm_own, sm_par, turns, blocks, dq, last):
    first = dq is None
    keys = [TILE if s == HOPS else 2 * TILE for s in offsets]
    here = pl.BlockSpec(memory_space=pltpu.VMEM)
    args = [query, other, dout, sm_own, sm_par, *turns, *blocks]
    if not first:
        args.append(dq)
    out_shape = [jax.ShapeDtypeStruct((2 * k, KV_COLS), jnp.bfloat16) for k in keys]
    if last:
        out_shape += [jax.ShapeDtypeStruct((TILE, Q_COLS), jnp.bfloat16)] * 2
    else:
        out_shape.append(jax.ShapeDtypeStruct((MY_HEADS, 2 * TILE, HEAD_SIZE), jnp.float32))
    flops = sum(10 * MY_HEADS * k * 2 * TILE * HEAD_SIZE for k in keys)
    return pl.pallas_call(
        functools.partial(pair_kernel, offsets, first, last),
        in_specs=[pl.BlockSpec(memory_space=pltpu.SMEM)] + [here] * len(args),
        out_specs=[here] * len(out_shape),
        out_shape=out_shape,
        scratch_shapes=[pltpu.VMEM((2 * TILE, k), jnp.float32) for k in keys],
        input_output_aliases={} if first or last else {len(args): len(out_shape) - 1},
        compiler_params=pltpu.CompilerParams(vmem_limit_bytes=24 * 1024 * 1024),
        cost_estimate=pl.CostEstimate(
            flops=flops,
            bytes_accessed=8 * 1024 * 1024,
            transcendentals=sum(MY_HEADS * k * 2 * TILE for k in keys),
        ),
    )(where, *args)


def add_back(arrived, part):
    if arrived.shape[0] < part.shape[0]:
        arrived = jnp.pad(arrived, ((0, part.shape[0] - arrived.shape[0]), (0, 0)))
    return (arrived.astype(jnp.float32) + part.astype(jnp.float32)).astype(jnp.bfloat16)


def row_kernel(column_ref, out_ref, dout_ref, lse_ref, tail_ref, own_ref, other_ref):
    step = pl.program_id(0)
    heads = QUERY_HEADS // 2
    ones = jnp.ones((8, HEAD_SIZE), jnp.bfloat16)
    rows = []
    for i in range(heads):
        cols = slice(i * HEAD_SIZE, (i + 1) * HEAD_SIZE)
        product = out_ref[:, cols].astype(jnp.float32) * dout_ref[:, cols].astype(jnp.float32)
        high = product.astype(jnp.bfloat16)
        low = (product - high.astype(jnp.float32)).astype(jnp.bfloat16)
        rows.append((nt(ones, high) + nt(ones, low))[:1])
    delta = jnp.concatenate(rows, axis=0)

    def fill(ref):
        ref[0:heads, :] = lse_ref[...] * (-LOG2E)
        ref[heads : 2 * heads, :] = delta
        ref[2 * heads : SMALL_ROWS, :] = tail_ref[...]

    @pl.when(step == column_ref[0])
    def _():
        fill(own_ref)

    @pl.when(step != column_ref[0])
    def _():
        fill(other_ref)


def row_values(column, out, dout, lse, seg_code, bitmap):
    tail = jnp.concatenate(
        [
            seg_code.astype(jnp.float32)[None, :],
            jnp.broadcast_to(bitmap.astype(jnp.float32)[None, :], (1, TILE)),
            jnp.zeros((SMALL_ROWS - 2 * MY_HEADS - 2, TILE), jnp.float32),
        ],
        axis=0,
    )
    wide = pl.BlockSpec((TILE, Q_COLS), lambda j, c: (0, j))
    return pl.pallas_call(
        row_kernel,
        grid_spec=pltpu.PrefetchScalarGridSpec(
            num_scalar_prefetch=1,
            grid=(2,),
            in_specs=[
                wide,
                wide,
                pl.BlockSpec((MY_HEADS, TILE), lambda j, c: (j, 0)),
                pl.BlockSpec((SMALL_ROWS - 2 * MY_HEADS, TILE), lambda j, c: (0, 0)),
            ],
            out_specs=[pl.BlockSpec((SMALL_ROWS, TILE), lambda j, c: (0, 0))] * 2,
        ),
        out_shape=[jax.ShapeDtypeStruct((SMALL_ROWS, TILE), jnp.float32)] * 2,
        cost_estimate=pl.CostEstimate(
            flops=4 * 8 * TILE * QUERY_HEADS * HEAD_SIZE, bytes_accessed=2**21, transcendentals=0
        ),
    )(column[None].astype(jnp.int32), out, dout, lse, tail)


def add_back(arrived, part):
    if arrived.shape[0] < part.shape[0]:
        arrived = jnp.pad(arrived, ((0, part.shape[0] - arrived.shape[0]), (0, 0)))
    return (arrived.astype(jnp.float32) + part.astype(jnp.float32)).astype(jnp.bfloat16)


def shards(query, key, value, out, dout, lse, segment, bitmap):
    place = lax.axis_index(AXES)
    column = place % 2
    where = jnp.stack([column, place]).astype(jnp.int32)

    def half(array, side, size, axis):
        return lax.dynamic_slice_in_dim(array, side * size, size, axis)

    odd = segment % 2 == 1
    seg_code = jnp.where(odd, (segment + 1) // 2, 0)
    seg_row = jnp.tile(seg_code.astype(jnp.bfloat16)[None, :], (1, MY_KV))
    seg_block = jnp.broadcast_to(seg_row, (SEG_ROWS, KV_COLS))
    sent = jnp.concatenate(
        [half(key, 1 - column, KV_COLS, 1), half(value, 1 - column, KV_COLS, 1), seg_block], axis=0
    )
    came = swap(sent)
    mine = jnp.concatenate(
        [half(key, column, KV_COLS, 1), half(value, column, KV_COLS, 1), seg_block], axis=0
    )
    tile0 = jnp.where(column == 0, mine, came)
    tile1 = jnp.where(column == 0, came, mine)
    seg_both = jnp.concatenate(
        [tile1[2 * TILE : 2 * TILE + 1], tile0[2 * TILE : 2 * TILE + SEG_ROWS - 1]], axis=0
    )
    block = jnp.concatenate([tile1[: 2 * TILE], seg_both, tile0[: 2 * TILE]], axis=0)

    sent_q = jnp.concatenate(
        [half(query, 1 - column, Q_COLS, 1), half(dout, 1 - column, Q_COLS, 1)], axis=0
    )
    smalls = row_values(column, out, dout, lse, seg_code, bitmap)
    sm_own = smalls[0]
    sm_par = swap(smalls[1])
    sent_q, sm_par = lax.optimization_barrier((sent_q, sm_par))
    other = swap(sent_q)

    blocks = [block]
    parts = {}
    dq = None
    ahead = {5: 4, 6: 5, 7: 6, 8: 7}
    behind = {8: 3, 7: 2, 6: 1, 5: 0}
    for hop in range(1, HOPS + 1):
        going = blocks[-1]
        if hop == HOPS:
            going = going[:HALF_ROWS]
        blocks.append(shift(going, 2))
        if hop in ahead:
            s = ahead[hop]
            parts[s], dq = pair_grads((s,), *common, [blocks[s]], dq, False)
            blocks[-1], dq = lax.optimization_barrier((blocks[-1], dq))
        if hop == 1:
            blocks[-1], sm_par = lax.optimization_barrier((blocks[-1], sm_par))
        if hop == 4:
            turns = turned(column, query, dout, other, sm_own, sm_par)
            common = (where, query, dout, other, sm_own, sm_par, turns)
    total, dq = pair_grads((HOPS,), *common, [blocks[HOPS]], dq, False)
    dq_came = None
    for hop in range(HOPS, 0, -1):
        arrived = shift(total, -2)
        if hop in behind:
            s = behind[hop]
            if s > 0:
                parts[s], dq = pair_grads((s,), *common, [blocks[s]], dq, False)
                arrived, dq = lax.optimization_barrier((arrived, dq))
            else:
                parts[s], dq_own, dq_par = pair_grads((s,), *common, [blocks[s]], dq, True)
                arrived, dq_par = lax.optimization_barrier((arrived, dq_par))
                dq_came = swap(dq_par)
        total = add_back(arrived, parts[hop - 1])

    tile1, tile0 = total[: 2 * TILE], total[2 * TILE :]
    mine = jnp.where(column == 0, tile0, tile1)
    came = swap(jnp.where(column == 0, tile1, tile0))
    low = jnp.where(column == 0, mine, came)
    high = jnp.where(column == 0, came, mine)
    dkey = jnp.concatenate([low[:TILE], high[:TILE]], axis=1)
    dvalue = jnp.concatenate([low[TILE:], high[TILE:]], axis=1)
    dquery = jnp.concatenate(
        [jnp.where(column == 0, dq_own, dq_came), jnp.where(column == 0, dq_came, dq_own)], axis=1
    )
    return dquery, dkey, dvalue


def solution(mesh):
    rows = P(AXES, None)
    return jax.shard_map(
        shards,
        mesh=mesh,
        in_specs=(rows, rows, rows, rows, rows, P(None, AXES), P(AXES), P(AXES)),
        out_specs=(rows, rows, rows),
        check_vma=False,
    )
```

time: 685 us -> 244 us (0.36)
  the two profiles are of different devices: /device:TPU:148 before, /device:TPU:4 now
where the time goes in v1:
time: 244 us
  starting transfers between devices  99.7 us (41%)
  waiting for transfers between devices  95.1 us (39%)
  Pallas kernels  41.9 us (17%)
  other arithmetic  4.75 us (2%)
    ppermute x16, waiting for transfers between devices, shift(): return lax.ppermute(array, AXES, pairs)  88 us
    ppermute x16, starting transfers between devices, shift(): return lax.ppermute(array, AXES, pairs)  85.4 us
    pallas_call x9, Pallas kernels, pair_grads(): pl.pallas_call(functools.partial(pair_kernel, offsets, first, last), in_s...  37.8 us
    ppermute x5, starting transfers between devices, swap(): return lax.ppermute(array, AXES, [(i, i ^ 1) for i in range(count)])  14.3 us
    ppermute x5, waiting for transfers between devices, swap(): return lax.ppermute(array, AXES, [(i, i ^ 1) for i in range(count)])  7.09 us
  transfers between devices with their start and end apart: 21, of which 16 were waited for; matrix products, arithmetic and copies ran while one was open for 1% of the time, Pallas kernels for 15%

profile of v1, /device:TPU:4, one launch (start us, length us, event | category | flops | bytes accessed | tf_op | source)
XLA Modules:
  0.0 243.5 jit_solution(14456442890999856350)
XLA Ops:
  12.4 4.2 %collective-permute-done.2 = bf16[272,256]{1,0:T(8,128)(2,1)S(1)} collective-permute-done((bf16[272,256]{1,0:T(8,128)(2,1)S(1)}, bf16[272,256]{1,0:T(8,128)(2,1)S(1)}, u32[]{:S(2)}, u32[]{:S(2)}) %collective-permute-start.2) | collective-permute-done | bytes 139296 | tf_op jit(solution)/shard_map/ppermute | solution.py:44
  23.3 10.6 %collective-permute-done.3.refs_8_ = bf16[528,256]{1,0:T(8,128)(2,1)S(1)} collective-permute-done((bf16[528,256]{1,0:T(8,128)(2,1)S(1)}, bf16[528,256]{1,0:T(8,128)(2,1)S(1)}, u32[]{:S(2)}, u32[]{:S(2)}) %collective-permute-start.3) | collective-permute-done | bytes 270368 | tf_op jit(solution)/shard_map/ppermute | solution.py:39
  35.8 12.2 %collective-permute-done.4.refs_8_ = bf16[528,256]{1,0:T(8,128)(2,1)S(1)} collective-permute-done((bf16[528,256]{1,0:T(8,128)(2,1)S(1)}, bf16[528,256]{1,0:T(8,128)(2,1)S(1)}, u32[]{:S(2)}, u32[]{:S(2)}) %collective-permute-start.4) | collective-permute-done | bytes 270368 | tf_op jit(solution)/shard_map/ppermute | solution.py:39
  49.9 11.9 %collective-permute-done.5.refs_8_ = bf16[528,256]{1,0:T(8,128)(2,1)S(1)} collective-permute-done((bf16[528,256]{1,0:T(8,128)(2,1)S(1)}, bf16[528,256]{1,0:T(8,128)(2,1)S(1)}, u32[]{:S(2)}, u32[]{:S(2)}) %collective-permute-start.5) | collective-permute-done | bytes 270368 | tf_op jit(solution)/shard_map/ppermute | solution.py:39
  63.8 12.5 %collective-permute-done.6.refs_8_ = bf16[528,256]{1,0:T(8,128)(2,1)S(1)} collective-permute-done((bf16[528,256]{1,0:T(8,128)(2,1)S(1)}, bf16[528,256]{1,0:T(8,128)(2,1)S(1)}, u32[]{:S(2)}, u32[]{:S(2)}) %collective-permute-start.6) | collective-permute-done | bytes 270368 | tf_op jit(solution)/shard_map/ppermute | solution.py:39
  79.0 4.3 %shard_map.105 = (bf16[512,256]{1,0:T(8,128)(2,1)S(1)}, f32[16,256,128]{2,1,0:T(8,128)S(1)}) custom-call(s32[2]{0:T(128)S(1)} %pad_add_fusion.where_ref, bf16[128,4096]{1,0:T(8,128)(2,1)S(1)} %copy-done.1, bf16[256,2048]{1,0:T(8,128)(2,1)S(1)} %collective-permute-done.1.q_par.refs_1_, bf16[128,4096]{1,0:T(8,128)(2,1)S(1)} %copy-done, ...), custom_call_target="tpu_custom_call" | custom-call | flops 1342177280 | bytes 8388608 | tf_op jit(solution)/shard_map/pallas_call | solution.py:226
  83.3 6.5 %collective-permute-done.7.refs_8_ = bf16[528,256]{1,0:T(8,128)(2,1)S(1)} collective-permute-done((bf16[528,256]{1,0:T(8,128)(2,1)S(1)}, bf16[528,256]{1,0:T(8,128)(2,1)S(1)}, u32[]{:S(2)}, u32[]{:S(2)}) %collective-permute-start.7) | collective-permute-done | bytes 270368 | tf_op jit(solution)/shard_map/ppermute | solution.py:39
  91.7 4.3 %shard_map.106 = (bf16[512,256]{1,0:T(8,128)(2,1)S(1)}, f32[16,256,128]{2,1,0:T(8,128)S(1)}) custom-call(s32[2]{0:T(128)S(1)} %pad_add_fusion.where_ref, bf16[128,4096]{1,0:T(8,128)(2,1)S(1)} %copy-done.1, bf16[256,2048]{1,0:T(8,128)(2,1)S(1)} %collective-permute-done.1.q_par.refs_1_, ...), custom_call_target="tpu_custom_call", output_to_operand_aliasing={{1}: (10, {})} | custom-call | flops 1342177280 | bytes 8388608 | tf_op jit(solution)/shard_map/pallas_call | solution.py:226
  96.1 7.4 %collective-permute-done.8.refs_8_ = bf16[528,256]{1,0:T(8,128)(2,1)S(1)} collective-permute-done((bf16[528,256]{1,0:T(8,128)(2,1)S(1)}, bf16[528,256]{1,0:T(8,128)(2,1)S(1)}, u32[]{:S(2)}, u32[]{:S(2)}) %collective-permute-start.8) | collective-permute-done | bytes 270368 | tf_op jit(solution)/shard_map/ppermute | solution.py:39
  105.4 4.3 %shard_map.107 = (bf16[512,256]{1,0:T(8,128)(2,1)S(1)}, f32[16,256,128]{2,1,0:T(8,128)S(1)}) custom-call(s32[2]{0:T(128)S(1)} %pad_add_fusion.where_ref, bf16[128,4096]{1,0:T(8,128)(2,1)S(1)} %copy-done.1, bf16[256,2048]{1,0:T(8,128)(2,1)S(1)} %collective-permute-done.1.q_par.refs_1_, ...), custom_call_target="tpu_custom_call", output_to_operand_aliasing={{1}: (10, {})} | custom-call | flops 1342177280 | bytes 8388608 | tf_op jit(solution)/shard_map/pallas_call | solution.py:226
  109.7 7.2 %collective-permute-done.9.refs_8_ = bf16[528,256]{1,0:T(8,128)(2,1)S(1)} collective-permute-done((bf16[528,256]{1,0:T(8,128)(2,1)S(1)}, bf16[528,256]{1,0:T(8,128)(2,1)S(1)}, u32[]{:S(2)}, u32[]{:S(2)}) %collective-permute-start.9) | collective-permute-done | bytes 270368 | tf_op jit(solution)/shard_map/ppermute | solution.py:39
  118.9 4.3 %shard_map.108 = (bf16[512,256]{1,0:T(8,128)(2,1)S(1)}, f32[16,256,128]{2,1,0:T(8,128)S(1)}) custom-call(s32[2]{0:T(128)S(1)} %pad_add_fusion.where_ref, bf16[128,4096]{1,0:T(8,128)(2,1)S(1)} %copy-done.1, bf16[256,2048]{1,0:T(8,128)(2,1)S(1)} %collective-permute-done.1.q_par.refs_1_, ...), custom_call_target="tpu_custom_call", output_to_operand_aliasing={{1}: (10, {})} | custom-call | flops 1342177280 | bytes 8388608 | tf_op jit(solution)/shard_map/pallas_call | solution.py:226
  123.2 5.8 %collective-permute-done.10.refs_8_ = bf16[272,256]{1,0:T(8,128)(2,1)S(1)} collective-permute-done((bf16[272,256]{1,0:T(8,128)(2,1)S(1)}, bf16[272,256]{1,0:T(8,128)(2,1)S(1)}, u32[]{:S(2)}, u32[]{:S(2)}) %collective-permute-start.10) | collective-permute-done | bytes 139296 | tf_op jit(solution)/shard_map/ppermute | solution.py:39
  136.0 4.3 %shard_map.110 = (bf16[512,256]{1,0:T(8,128)(2,1)S(1)}, f32[16,256,128]{2,1,0:T(8,128)S(1)}) custom-call(s32[2]{0:T(128)S(1)} %pad_add_fusion.where_ref, bf16[128,4096]{1,0:T(8,128)(2,1)S(1)} %copy-done.1, bf16[256,2048]{1,0:T(8,128)(2,1)S(1)} %collective-permute-done.1.q_par.refs_1_, ...), custom_call_target="tpu_custom_call", output_to_operand_aliasing={{1}: (10, {})} | custom-call | flops 1342177280 | bytes 8388608 | tf_op jit(solution)/shard_map/pallas_call | solution.py:226
  140.4 7.5 %collective-permute-start.12 = (bf16[512,256]{1,0:T(8,128)(2,1)S(1)}, bf16[512,256]{1,0:T(8,128)(2,1)S(1)}, u32[]{:S(2)}, u32[]{:S(2)}) collective-permute-start(bf16[512,256]{1,0:T(8,128)(2,1)S(1)} %add_convert_fusion.7), channel_id=1, source_target_pairs={{2,0},{3,1},{4,2},{5,3},{6,4},{7,5},{8,6},{9,7},{10,8},{11,9},{12,... | collective-permute-start | bytes 786440 | tf_op jit(solution)/shard_map/ppermute | solution.py:39
  147.9 4.3 %shard_map.111 = (bf16[512,256]{1,0:T(8,128)(2,1)S(1)}, f32[16,256,128]{2,1,0:T(8,128)S(1)}) custom-call(s32[2]{0:T(128)S(1)} %pad_add_fusion.where_ref, bf16[128,4096]{1,0:T(8,128)(2,1)S(1)} %copy-done.1, bf16[256,2048]{1,0:T(8,128)(2,1)S(1)} %collective-permute-done.1.q_par.refs_1_, ...), custom_call_target="tpu_custom_call", output_to_operand_aliasing={{1}: (10, {})} | custom-call | flops 1342177280 | bytes 8388608 | tf_op jit(solution)/shard_map/pallas_call | solution.py:226
  153.1 9.5 %collective-permute-start.13 = (bf16[512,256]{1,0:T(8,128)(2,1)S(1)}, bf16[512,256]{1,0:T(8,128)(2,1)S(1)}, u32[]{:S(2)}, u32[]{:S(2)}) collective-permute-start(bf16[512,256]{1,0:T(8,128)(2,1)S(1)} %add_convert_fusion.6), channel_id=1, source_target_pairs={{2,0},{3,1},{4,2},{5,3},{6,4},{7,5},{8,6},{9,7},{10,8},{11,9},{12,... | collective-permute-start | bytes 786440 | tf_op jit(solution)/shard_map/ppermute | solution.py:39
  162.6 4.3 %shard_map.112 = (bf16[512,256]{1,0:T(8,128)(2,1)S(1)}, f32[16,256,128]{2,1,0:T(8,128)S(1)}) custom-call(s32[2]{0:T(128)S(1)} %pad_add_fusion.where_ref, bf16[128,4096]{1,0:T(8,128)(2,1)S(1)} %copy-done.1, bf16[256,2048]{1,0:T(8,128)(2,1)S(1)} %collective-permute-done.1.q_par.refs_1_, ...), custom_call_target="tpu_custom_call", output_to_operand_aliasing={{1}: (10, {})} | custom-call | flops 1342177280 | bytes 8388608 | tf_op jit(solution)/shard_map/pallas_call | solution.py:226
  167.1 9.2 %collective-permute-start.14 = (bf16[512,256]{1,0:T(8,128)(2,1)S(1)}, bf16[512,256]{1,0:T(8,128)(2,1)S(1)}, u32[]{:S(2)}, u32[]{:S(2)}) collective-permute-start(bf16[512,256]{1,0:T(8,128)(2,1)S(1)} %add_convert_fusion.5), channel_id=1, source_target_pairs={{2,0},{3,1},{4,2},{5,3},{6,4},{7,5},{8,6},{9,7},{10,8},{11,9},{12,... | collective-permute-start | bytes 786440 | tf_op jit(solution)/shard_map/ppermute | solution.py:39
  176.2 4.3 %shard_map.113 = (bf16[512,256]{1,0:T(8,128)(2,1)S(1)}, bf16[128,2048]{1,0:T(8,128)(2,1)S(1)}, bf16[128,2048]{1,0:T(8,128)(2,1)S(1)}) custom-call(s32[2]{0:T(128)S(1)} %pad_add_fusion.where_ref, bf16[128,4096]{1,0:T(8,128)(2,1)S(1)} %copy-done.1, bf16[256,2048]{1,0:T(8,128)(2,1)S(1)} %collective-permute-done.1.q_par.refs_1_, bf16[128,4096]{1,0:T(8,128)(2,1)S(1)} %copy-done, ...), custom_call_target="tpu_custom_call" | custom-call | flops 1342177280 | bytes 8388608 | tf_op jit(solution)/shard_map/pallas_call | solution.py:226
  181.2 9.5 %collective-permute-start.16 = (bf16[512,256]{1,0:T(8,128)(2,1)S(1)}, bf16[512,256]{1,0:T(8,128)(2,1)S(1)}, u32[]{:S(2)}, u32[]{:S(2)}) collective-permute-start(bf16[512,256]{1,0:T(8,128)(2,1)S(1)} %add_convert_fusion.4), channel_id=1, source_target_pairs={{2,0},{3,1},{4,2},{5,3},{6,4},{7,5},{8,6},{9,7},{10,8},{11,9},{12,... | collective-permute-start | bytes 786440 | tf_op jit(solution)/shard_map/ppermute | solution.py:39
  194.7 9.6 %collective-permute-start.17 = (bf16[512,256]{1,0:T(8,128)(2,1)S(1)}, bf16[512,256]{1,0:T(8,128)(2,1)S(1)}, u32[]{:S(2)}, u32[]{:S(2)}) collective-permute-start(bf16[512,256]{1,0:T(8,128)(2,1)S(1)} %add_convert_fusion.3), channel_id=1, source_target_pairs={{2,0},{3,1},{4,2},{5,3},{6,4},{7,5},{8,6},{9,7},{10,8},{11,9},{12,... | collective-permute-start | bytes 786440 | tf_op jit(solution)/shard_map/ppermute | solution.py:39
  208.3 9.5 %collective-permute-start.18 = (bf16[512,256]{1,0:T(8,128)(2,1)S(1)}, bf16[512,256]{1,0:T(8,128)(2,1)S(1)}, u32[]{:S(2)}, u32[]{:S(2)}) collective-permute-start(bf16[512,256]{1,0:T(8,128)(2,1)S(1)} %add_convert_fusion.2), channel_id=1, source_target_pairs={{2,0},{3,1},{4,2},{5,3},{6,4},{7,5},{8,6},{9,7},{10,8},{11,9},{12,... | collective-permute-start | bytes 786440 | tf_op jit(solution)/shard_map/ppermute | solution.py:39
  221.8 9.5 %collective-permute-start.19 = (bf16[512,256]{1,0:T(8,128)(2,1)S(1)}, bf16[512,256]{1,0:T(8,128)(2,1)S(1)}, u32[]{:S(2)}, u32[]{:S(2)}) collective-permute-start(bf16[512,256]{1,0:T(8,128)(2,1)S(1)} %add_convert_fusion.1), channel_id=1, source_target_pairs={{2,0},{3,1},{4,2},{5,3},{6,4},{7,5},{8,6},{9,7},{10,8},{11,9},{12,... | collective-permute-start | bytes 786440 | tf_op jit(solution)/shard_map/ppermute | solution.py:39
  (74 shorter events, 64.4 us)
Async XLA Ops:
  0.6 11.6 %copy-start = (bf16[128,4096]{1,0:T(8,128)(2,1)S(1)}, bf16[128,4096]{1,0:T(8,128)(2,1)}, u32[]{:S(2)}) copy-start(bf16[128,4096]{1,0:T(8,128)(2,1)} %refs_2_.17) | copy-start | bytes 3145732
  0.7 11.6 %copy-start.1 = (bf16[128,4096]{1,0:T(8,128)(2,1)S(1)}, bf16[128,4096]{1,0:T(8,128)(2,1)}, u32[]{:S(2)}) copy-start(bf16[128,4096]{1,0:T(8,128)(2,1)} %refs_0_.17) | copy-start | bytes 3145732
  6.3 14.3 %collective-permute-start = (f32[40,128]{1,0:T(8,128)}, f32[40,128]{1,0:T(8,128)S(1)}, u32[]{:S(2)}, u32[]{:S(2)}) collective-permute-start(f32[40,128]{1,0:T(8,128)} %get-tuple-element.47), channel_id=1, source_target_pairs={{0,1},{1,0},{2,3},{3,2},{4,5},{5,4},{6,7},{7,6},{8,9},{9,8},{10,11... | collective-permute-start | bytes 61448 | tf_op jit(solution)/shard_map/ppermute | solution.py:44
  9.5 7.0 %collective-permute-start.2 = (bf16[272,256]{1,0:T(8,128)(2,1)S(1)}, bf16[272,256]{1,0:T(8,128)(2,1)S(1)}, u32[]{:S(2)}, u32[]{:S(2)}) collective-permute-start(bf16[272,256]{1,0:T(8,128)(2,1)S(1)} %pad_maximum_fusion.4), channel_id=1, source_target_pairs={{0,1},{1,0},{2,3},{3,2},{4,5},{5,4},{6,7},{7,6},{8,9},{9,8},{10,11... | collective-permute-start | bytes 417800 | tf_op jit(solution)/shard_map/ppermute | solution.py:44
  12.4 65.9 %copy-start.2 = (f32[40,128]{1,0:T(8,128)S(1)}, f32[40,128]{1,0:T(8,128)}, u32[]{:S(2)}) copy-start(f32[40,128]{1,0:T(8,128)} %get-tuple-element.49.sm_own.refs_3_) | copy-start | bytes 61444
  16.6 17.3 %collective-permute-start.3 = (bf16[528,256]{1,0:T(8,128)(2,1)S(1)}, bf16[528,256]{1,0:T(8,128)(2,1)S(1)}, u32[]{:S(2)}, u32[]{:S(2)}) collective-permute-start(bf16[528,256]{1,0:T(8,128)(2,1)S(1)} %pad_maximum_fusion.2.refs_8_), channel_id=1, source_target_pairs={{0,2},{1,3},{2,4},{3,5},{4,6},{5,7},{6,8},{7,9},{8,10},{9,11},{10,... | collective-permute-start | bytes 811016 | tf_op jit(solution)/shard_map/ppermute | solution.py:39
  20.6 57.7 %collective-permute-start.1 = (bf16[256,2048]{1,0:T(8,128)(2,1)S(1)}, bf16[256,2048]{1,0:T(8,128)(2,1)S(1)}, u32[]{:S(2)}, u32[]{:S(2)}) collective-permute-start(bf16[256,2048]{1,0:T(8,128)(2,1)S(1)} %pad_maximum_fusion), channel_id=1, source_target_pairs={{0,1},{1,0},{2,3},{3,2},{4,5},{5,4},{6,7},{7,6},{8,9},{9,8},{10,11... | collective-permute-start | bytes 3145736 | tf_op jit(solution)/shard_map/ppermute | solution.py:44
  33.9 14.1 %collective-permute-start.4 = (bf16[528,256]{1,0:T(8,128)(2,1)S(1)}, bf16[528,256]{1,0:T(8,128)(2,1)S(1)}, u32[]{:S(2)}, u32[]{:S(2)}) collective-permute-start(bf16[528,256]{1,0:T(8,128)(2,1)S(1)} %collective-permute-done.3.refs_8_), channel_id=1, source_target_pairs={{0,2},{1,3},{2,4},{3,5},{4,6},{5,7},{6,8},{7,9},{8,10},{9,11},{10,... | collective-permute-start | bytes 811016 | tf_op jit(solution)/shard_map/ppermute | solution.py:39
  48.0 13.8 %collective-permute-start.5 = (bf16[528,256]{1,0:T(8,128)(2,1)S(1)}, bf16[528,256]{1,0:T(8,128)(2,1)S(1)}, u32[]{:S(2)}, u32[]{:S(2)}) collective-permute-start(bf16[528,256]{1,0:T(8,128)(2,1)S(1)} %collective-permute-done.4.refs_8_), channel_id=1, source_target_pairs={{0,2},{1,3},{2,4},{3,5},{4,6},{5,7},{6,8},{7,9},{8,10},{9,11},{10,... | collective-permute-start | bytes 811016 | tf_op jit(solution)/shard_map/ppermute | solution.py:39
  61.8 14.4 %collective-permute-start.6 = (bf16[528,256]{1,0:T(8,128)(2,1)S(1)}, bf16[528,256]{1,0:T(8,128)(2,1)S(1)}, u32[]{:S(2)}, u32[]{:S(2)}) collective-permute-start(bf16[528,256]{1,0:T(8,128)(2,1)S(1)} %collective-permute-done.5.refs_8_), channel_id=1, source_target_pairs={{0,2},{1,3},{2,4},{3,5},{4,6},{5,7},{6,8},{7,9},{8,10},{9,11},{10,... | collective-permute-start | bytes 811016 | tf_op jit(solution)/shard_map/ppermute | solution.py:39
  76.3 13.6 %collective-permute-start.7 = (bf16[528,256]{1,0:T(8,128)(2,1)S(1)}, bf16[528,256]{1,0:T(8,128)(2,1)S(1)}, u32[]{:S(2)}, u32[]{:S(2)}) collective-permute-start(bf16[528,256]{1,0:T(8,128)(2,1)S(1)} %collective-permute-done.6.refs_8_), channel_id=1, source_target_pairs={{0,2},{1,3},{2,4},{3,5},{4,6},{5,7},{6,8},{7,9},{8,10},{9,11},{10,... | collective-permute-start | bytes 811016 | tf_op jit(solution)/shard_map/ppermute | solution.py:39
  89.8 13.6 %collective-permute-start.8 = (bf16[528,256]{1,0:T(8,128)(2,1)S(1)}, bf16[528,256]{1,0:T(8,128)(2,1)S(1)}, u32[]{:S(2)}, u32[]{:S(2)}) collective-permute-start(bf16[528,256]{1,0:T(8,128)(2,1)S(1)} %collective-permute-done.7.refs_8_), channel_id=1, source_target_pairs={{0,2},{1,3},{2,4},{3,5},{4,6},{5,7},{6,8},{7,9},{8,10},{9,11},{10,... | collective-permute-start | bytes 811016 | tf_op jit(solution)/shard_map/ppermute | solution.py:39
  103.4 13.5 %collective-permute-start.9 = (bf16[528,256]{1,0:T(8,128)(2,1)S(1)}, bf16[528,256]{1,0:T(8,128)(2,1)S(1)}, u32[]{:S(2)}, u32[]{:S(2)}) collective-permute-start(bf16[528,256]{1,0:T(8,128)(2,1)S(1)} %collective-permute-done.8.refs_8_), channel_id=1, source_target_pairs={{0,2},{1,3},{2,4},{3,5},{4,6},{5,7},{6,8},{7,9},{8,10},{9,11},{10,... | collective-permute-start | bytes 811016 | tf_op jit(solution)/shard_map/ppermute | solution.py:39
  117.0 12.1 %collective-permute-start.10 = (bf16[272,256]{1,0:T(8,128)(2,1)S(1)}, bf16[272,256]{1,0:T(8,128)(2,1)S(1)}, u32[]{:S(2)}, u32[]{:S(2)}) collective-permute-start(bf16[272,256]{1,0:T(8,128)(2,1)S(1)} %slice.35), channel_id=1, source_target_pairs={{0,2},{1,3},{2,4},{3,5},{4,6},{5,7},{6,8},{7,9},{8,10},{9,11},{10,... | collective-permute-start | bytes 417800 | tf_op jit(solution)/shard_map/ppermute | solution.py:39
  132.2 8.1 %collective-permute-start.11 = (bf16[256,256]{1,0:T(8,128)(2,1)S(1)}, bf16[256,256]{1,0:T(8,128)(2,1)S(1)}, u32[]{:S(2)}, u32[]{:S(2)}) collective-permute-start(bf16[256,256]{1,0:T(8,128)(2,1)S(1)} %get-tuple-element.68), channel_id=1, source_target_pairs={{2,0},{3,1},{4,2},{5,3},{6,4},{7,5},{8,6},{9,7},{10,8},{11,9},{12,... | collective-permute-start | bytes 393224 | tf_op jit(solution)/shard_map/ppermute | solution.py:39
  140.4 12.6 %collective-permute-start.12 = (bf16[512,256]{1,0:T(8,128)(2,1)S(1)}, bf16[512,256]{1,0:T(8,128)(2,1)S(1)}, u32[]{:S(2)}, u32[]{:S(2)}) collective-permute-start(bf16[512,256]{1,0:T(8,128)(2,1)S(1)} %add_convert_fusion.7), channel_id=1, source_target_pairs={{2,0},{3,1},{4,2},{5,3},{6,4},{7,5},{8,6},{9,7},{10,8},{11,9},{12,... | collective-permute-start | bytes 786440 | tf_op jit(solution)/shard_map/ppermute | solution.py:39
  153.1 13.9 %collective-permute-start.13 = (bf16[512,256]{1,0:T(8,128)(2,1)S(1)}, bf16[512,256]{1,0:T(8,128)(2,1)S(1)}, u32[]{:S(2)}, u32[]{:S(2)}) collective-permute-start(bf16[512,256]{1,0:T(8,128)(2,1)S(1)} %add_convert_fusion.6), channel_id=1, source_target_pairs={{2,0},{3,1},{4,2},{5,3},{6,4},{7,5},{8,6},{9,7},{10,8},{11,9},{12,... | collective-permute-start | bytes 786440 | tf_op jit(solution)/shard_map/ppermute | solution.py:39
  167.1 14.1 %collective-permute-start.14 = (bf16[512,256]{1,0:T(8,128)(2,1)S(1)}, bf16[512,256]{1,0:T(8,128)(2,1)S(1)}, u32[]{:S(2)}, u32[]{:S(2)}) collective-permute-start(bf16[512,256]{1,0:T(8,128)(2,1)S(1)} %add_convert_fusion.5), channel_id=1, source_target_pairs={{2,0},{3,1},{4,2},{5,3},{6,4},{7,5},{8,6},{9,7},{10,8},{11,9},{12,... | collective-permute-start | bytes 786440 | tf_op jit(solution)/shard_map/ppermute | solution.py:39
  181.2 13.4 %collective-permute-start.16 = (bf16[512,256]{1,0:T(8,128)(2,1)S(1)}, bf16[512,256]{1,0:T(8,128)(2,1)S(1)}, u32[]{:S(2)}, u32[]{:S(2)}) collective-permute-start(bf16[512,256]{1,0:T(8,128)(2,1)S(1)} %add_convert_fusion.4), channel_id=1, source_target_pairs={{2,0},{3,1},{4,2},{5,3},{6,4},{7,5},{8,6},{9,7},{10,8},{11,9},{12,... | collective-permute-start | bytes 786440 | tf_op jit(solution)/shard_map/ppermute | solution.py:39
  194.7 13.5 %collective-permute-start.17 = (bf16[512,256]{1,0:T(8,128)(2,1)S(1)}, bf16[512,256]{1,0:T(8,128)(2,1)S(1)}, u32[]{:S(2)}, u32[]{:S(2)}) collective-permute-start(bf16[512,256]{1,0:T(8,128)(2,1)S(1)} %add_convert_fusion.3), channel_id=1, source_target_pairs={{2,0},{3,1},{4,2},{5,3},{6,4},{7,5},{8,6},{9,7},{10,8},{11,9},{12,... | collective-permute-start | bytes 786440 | tf_op jit(solution)/shard_map/ppermute | solution.py:39
  204.4 27.0 %collective-permute-start.15 = (bf16[128,2048]{1,0:T(8,128)(2,1)S(1)}, bf16[128,2048]{1,0:T(8,128)(2,1)S(1)}, u32[]{:S(2)}, u32[]{:S(2)}) collective-permute-start(bf16[128,2048]{1,0:T(8,128)(2,1)S(1)} %get-tuple-element.84), channel_id=1, source_target_pairs={{0,1},{1,0},{2,3},{3,2},{4,5},{5,4},{6,7},{7,6},{8,9},{9,8},{10,11... | collective-permute-start | bytes 1572872 | tf_op jit(solution)/shard_map/ppermute | solution.py:44
  208.3 13.4 %collective-permute-start.18 = (bf16[512,256]{1,0:T(8,128)(2,1)S(1)}, bf16[512,256]{1,0:T(8,128)(2,1)S(1)}, u32[]{:S(2)}, u32[]{:S(2)}) collective-permute-start(bf16[512,256]{1,0:T(8,128)(2,1)S(1)} %add_convert_fusion.2), channel_id=1, source_target_pairs={{2,0},{3,1},{4,2},{5,3},{6,4},{7,5},{8,6},{9,7},{10,8},{11,9},{12,... | collective-permute-start | bytes 786440 | tf_op jit(solution)/shard_map/ppermute | solution.py:39
  221.8 13.4 %collective-permute-start.19 = (bf16[512,256]{1,0:T(8,128)(2,1)S(1)}, bf16[512,256]{1,0:T(8,128)(2,1)S(1)}, u32[]{:S(2)}, u32[]{:S(2)}) collective-permute-start(bf16[512,256]{1,0:T(8,128)(2,1)S(1)} %add_convert_fusion.1), channel_id=1, source_target_pairs={{2,0},{3,1},{4,2},{5,3},{6,4},{7,5},{8,6},{9,7},{10,8},{11,9},{12,... | collective-permute-start | bytes 786440 | tf_op jit(solution)/shard_map/ppermute | solution.py:39
  235.3 6.9 %collective-permute-start.20 = (bf16[256,256]{1,0:T(8,128)(2,1)S(1)}, bf16[256,256]{1,0:T(8,128)(2,1)S(1)}, u32[]{:S(2)}, u32[]{:S(2)}) collective-permute-start(bf16[256,256]{1,0:T(8,128)(2,1)S(1)} %broadcast_select_fusion.5), channel_id=1, source_target_pairs={{0,1},{1,0},{2,3},{3,2},{4,5},{5,4},{6,7},{7,6},{8,9},{9,8},{10,11... | collective-permute-start | bytes 393224 | tf_op jit(solution)/shard_map/ppermute | solution.py:44
  (2 other events, 17.5 us)

commit v2 on v1

--- a/solution.py
+++ b/solution.py
@@ -35,8 +35,7 @@
 
 def shift(array, by):
     count = lax.axis_size(AXES)
-    pairs = [(i, i + by) for i in range(count) if 0 <= i + by < count]
-    return lax.ppermute(array, AXES, pairs)
+    return lax.ppermute(array, AXES, [(i, (i + by) % count) for i in range(count)])
 
 
 def swap(array):
@@ -239,10 +238,14 @@
     )(where, *args)
 
 
+def sum_up(*arrays):
+    return sum(array.astype(jnp.float32) for array in arrays).astype(jnp.bfloat16)
+
+
 def add_back(arrived, part):
-    if arrived.shape[0] < part.shape[0]:
-        arrived = jnp.pad(arrived, ((0, part.shape[0] - arrived.shape[0]), (0, 0)))
-    return (arrived.astype(jnp.float32) + part.astype(jnp.float32)).astype(jnp.bfloat16)
+    if part.shape[0] < arrived.shape[0]:
+        part = jnp.pad(part, ((0, arrived.shape[0] - part.shape[0]), (0, 0)))
+    return sum_up(arrived, part)
 
 
 def row_kernel(column_ref, out_ref, dout_ref, lse_ref, tail_ref, own_ref, other_ref):
@@ -302,10 +305,8 @@
     )(column[None].astype(jnp.int32), out, dout, lse, tail)
 
 
-def add_back(arrived, part):
-    if arrived.shape[0] < part.shape[0]:
-        arrived = jnp.pad(arrived, ((0, part.shape[0] - arrived.shape[0]), (0, 0)))
-    return (arrived.astype(jnp.float32) + part.astype(jnp.float32)).astype(jnp.bfloat16)
+def tie(first, second):
+    return lax.optimization_barrier((first, second))
 
 
 def shards(query, key, value, out, dout, lse, segment, bitmap):
@@ -323,6 +324,7 @@
     sent = jnp.concatenate(
         [half(key, 1 - column, KV_COLS, 1), half(value, 1 - column, KV_COLS, 1), seg_block], axis=0
     )
+    lse, sent = tie(lse, sent)
     came = swap(sent)
     mine = jnp.concatenate(
         [half(key, column, KV_COLS, 1), half(value, column, KV_COLS, 1), seg_block], axis=0
@@ -343,39 +345,63 @@
     sent_q, sm_par = lax.optimization_barrier((sent_q, sm_par))
     other = swap(sent_q)
 
-    blocks = [block]
+    blocks = {0: block}
+    blocks[1] = shift(block, 2)
+    far_block, sm_par = tie(block, sm_par)
+    far_block, sent_q = tie(far_block, sent_q)
+    blocks[8] = shift(far_block, 2 * HOPS)
+    blocks[2] = shift(blocks[1], 2)
+
     parts = {}
     dq = None
-    ahead = {5: 4, 6: 5, 7: 6, 8: 7}
-    behind = {8: 3, 7: 2, 6: 1, 5: 0}
-    for hop in range(1, HOPS + 1):
-        going = blocks[-1]
-        if hop == HOPS:
-            going = going[:HALF_ROWS]
-        blocks.append(shift(going, 2))
-        if hop in ahead:
-            s = ahead[hop]
-            parts[s], dq = pair_grads((s,), *common, [blocks[s]], dq, False)
-            blocks[-1], dq = lax.optimization_barrier((blocks[-1], dq))
-        if hop == 1:
-            blocks[-1], sm_par = lax.optimization_barrier((blocks[-1], sm_par))
-        if hop == 4:
-            turns = turned(column, query, dout, other, sm_own, sm_par)
-            common = (where, query, dout, other, sm_own, sm_par, turns)
-    total, dq = pair_grads((HOPS,), *common, [blocks[HOPS]], dq, False)
-    dq_came = None
-    for hop in range(HOPS, 0, -1):
-        arrived = shift(total, -2)
-        if hop in behind:
-            s = behind[hop]
-            if s > 0:
-                parts[s], dq = pair_grads((s,), *common, [blocks[s]], dq, False)
-                arrived, dq = lax.optimization_barrier((arrived, dq))
-            else:
-                parts[s], dq_own, dq_par = pair_grads((s,), *common, [blocks[s]], dq, True)
-                arrived, dq_par = lax.optimization_barrier((arrived, dq_par))
-                dq_came = swap(dq_par)
-        total = add_back(arrived, parts[hop - 1])
+    turns = turned(column, query, dout, other, sm_own, sm_par)
+
+    def work(offsets, last=False):
+        nonlocal dq
+        common = (where, query, dout, other, sm_own, sm_par, turns)
+        given = [blocks[s][:HALF_ROWS] if s == HOPS else blocks[s] for s in offsets]
+        made = pair_grads(offsets, *common, given, dq, last)
+        parts.update(zip(offsets, made))
+        dq = made[len(offsets) :] if last else made[-1]
+
+    def then(array):
+        nonlocal dq
+        array, dq = tie(array, dq)
+        return array
+
+    work((0, 1))
+    blocks[8] = then(blocks[8])
+    blocks[7] = shift(blocks[8], -2)
+    blocks[2], blocks[8] = tie(blocks[2], blocks[8])
+    blocks[3] = shift(blocks[2], 2)
+    work((8,))
+    work((2,))
+    blocks[7] = then(blocks[7])
+    blocks[3] = then(blocks[3])
+    blocks[6] = shift(blocks[7], -2)
+    blocks[4] = shift(blocks[3], 2)
+    work((7,))
+    work((3,))
+    blocks[6] = then(blocks[6])
+    blocks[4] = then(blocks[4])
+    blocks[5] = shift(blocks[6], -2)
+    work((6,))
+    work((4,))
+    near = shift(parts[4], -2)
+    blocks[5] = then(blocks[5])
+    work((5,), True)
+    dq_own, dq_par = dq
+    far = shift(parts[5], 2)
+    near, dq_par = tie(near, dq_par)
+    near = shift(add_back(near, parts[3]), -2)
+    dq_came = swap(dq_par)
+    far = shift(add_back(far, parts[6]), 2)
+    near = shift(add_back(near, parts[2]), -2)
+    far = shift(add_back(far, parts[7]), 2)
+    far, near = tie(far, near)
+    far = shift(add_back(far, parts[8]), -2 * HOPS)
+    near = shift(add_back(near, parts[1]), -2)
+    total = sum_up(near, parts[0], far)
 
     tile1, tile0 = total[: 2 * TILE], total[2 * TILE :]
     mine = jnp.where(column == 0, tile0, tile1)

time: 244 us -> 202 us (0.83)
  the two profiles are of different devices: /device:TPU:4 before, /device:TPU:2 now
where the time goes in v2:
time: 202 us; the launch traced here: 201 us
  starting transfers between devices  95.4 us (47%)
  waiting for transfers between devices  55.6 us (28%)
  Pallas kernels  40.8 us (20%)
  other arithmetic  6.33 us (3%)
    ppermute x16, starting transfers between devices, shift(): lax.ppermute(array, AXES, [(i, (i + by) % count) for i in range(count)])  77.2 us
    ppermute x16, waiting for transfers between devices, shift(): lax.ppermute(array, AXES, [(i, (i + by) % count) for i in range(count)])  49.6 us
    pallas_call x8, Pallas kernels, pair_grads(): pl.pallas_call(functools.partial(pair_kernel, offsets, first, last), in_s...  36.7 us
    ppermute x5, starting transfers between devices, swap(): return lax.ppermute(array, AXES, [(i, i ^ 1) for i in range(count)])  18.3 us
    ppermute x5, waiting for transfers between devices, swap(): return lax.ppermute(array, AXES, [(i, i ^ 1) for i in range(count)])  5.95 us
  transfers between devices with their start and end apart: 21, of which 11 were waited for; matrix products, arithmetic and copies ran while one was open for 2% of the time, Pallas kernels for 20%

profile of v2, /device:TPU:2, one launch (start us, length us, event | category | flops | bytes accessed | tf_op | source)
XLA Modules:
  0.0 201.2 jit_solution(11020718528858510457)
XLA Ops:
  3.1 7.8 %collective-permute-start.2 = (bf16[272,256]{1,0:T(8,128)(2,1)}, bf16[272,256]{1,0:T(8,128)(2,1)S(1)}, u32[]{:S(2)}, u32[]{:S(2)}) collective-permute-start(bf16[272,256]{1,0:T(8,128)(2,1)} %pad_maximum_fusion.4), channel_id=1, source_target_pairs={{0,1},{1,0},{2,3},{3,2},{4,5},{5,4},{6,7},{7,6},{8,9},{9,8},{10,11... | collective-permute-start | bytes 417800 | tf_op jit(solution)/shard_map/ppermute | solution.py:43
  12.4 3.3 %shard_map.103 = (f32[40,128]{1,0:T(8,128)}, f32[40,128]{1,0:T(8,128)}) custom-call(s32[1]{0:T(128)} %bitcast.column_ref, bf16[128,4096]{1,0:T(8,128)(2,1)} %out_ref.1, bf16[128,4096]{1,0:T(8,128)(2,1)} %refs_2_.15, f32[32,128]{1,0:T(8,128)} %lse_ref, f32[8,128]{1,0:T(8,128)} %maximum_maximum_fusion.tail_ref), custom_call_target="tpu_custom_call" | custom-call | flops 16777216 | bytes 2097152 | tf_op jit(solution)/shard_map/pallas_call | solution.py:288
  18.8 3.0 %collective-permute-done.sm_par.refs_4_ = f32[40,128]{1,0:T(8,128)S(1)} collective-permute-done((f32[40,128]{1,0:T(8,128)}, f32[40,128]{1,0:T(8,128)S(1)}, u32[]{:S(2)}, u32[]{:S(2)}) %collective-permute-start) | collective-permute-done | bytes 20512 | tf_op jit(solution)/shard_map/ppermute | solution.py:43
  25.9 12.6 %collective-permute-start.3 = (bf16[528,256]{1,0:T(8,128)(2,1)S(1)}, bf16[528,256]{1,0:T(8,128)(2,1)S(1)}, u32[]{:S(2)}, u32[]{:S(2)}) collective-permute-start(bf16[528,256]{1,0:T(8,128)(2,1)S(1)} %pad_maximum_fusion.2.refs_8_), channel_id=1, source_target_pairs={{0,16},{1,17},{2,18},{3,19},{4,20},{5,21},{6,22},{7,23},{8,24},{9,... | collective-permute-start | bytes 811016 | tf_op jit(solution)/shard_map/ppermute | solution.py:38
  42.8 7.6 %shard_map.105 = (bf16[512,256]{1,0:T(8,128)(2,1)S(1)}, bf16[512,256]{1,0:T(8,128)(2,1)S(1)}, f32[16,256,128]{2,1,0:T(8,128)S(1)}) custom-call(s32[2]{0:T(128)S(1)} %pad_add_fusion.where_ref, bf16[128,4096]{1,0:T(8,128)(2,1)S(1)} %copy-done.1, bf16[256,2048]{1,0:T(8,128)(2,1)S(1)} %collective-permute-done.1.q_par.refs_1_, bf16[128,4096]{1,0:T(8,128)(2,1)S(1)} %copy-done, ...), custom_call_target="tpu_custom_call" | custom-call | flops 2684354560 | bytes 8388608 | tf_op jit(solution)/shard_map/pallas_call | solution.py:225
  50.4 10.8 %collective-permute-done.3 = bf16[528,256]{1,0:T(8,128)(2,1)S(1)} collective-permute-done((bf16[528,256]{1,0:T(8,128)(2,1)S(1)}, bf16[528,256]{1,0:T(8,128)(2,1)S(1)}, u32[]{:S(2)}, u32[]{:S(2)}) %collective-permute-start.3) | collective-permute-done | bytes 270368 | tf_op jit(solution)/shard_map/ppermute | solution.py:38
  61.2 9.3 %collective-permute-start.5 = (bf16[528,256]{1,0:T(8,128)(2,1)S(1)}, bf16[528,256]{1,0:T(8,128)(2,1)S(1)}, u32[]{:S(2)}, u32[]{:S(2)}) collective-permute-start(bf16[528,256]{1,0:T(8,128)(2,1)S(1)} %collective-permute-done.3), channel_id=1, source_target_pairs={{0,510},{1,511},{2,0},{3,1},{4,2},{5,3},{6,4},{7,5},{8,6},{9,7},{1... | collective-permute-start | bytes 811016 | tf_op jit(solution)/shard_map/ppermute | solution.py:38
  72.9 3.2 %shard_map.106 = (bf16[256,256]{1,0:T(8,128)(2,1)S(1)}, f32[16,256,128]{2,1,0:T(8,128)S(1)}) custom-call(s32[2]{0:T(128)S(1)} %pad_add_fusion.where_ref, bf16[128,4096]{1,0:T(8,128)(2,1)S(1)} %copy-done.1, bf16[256,2048]{1,0:T(8,128)(2,1)S(1)} %collective-permute-done.1.q_par.refs_1_, ...), custom_call_target="tpu_custom_call", output_to_operand_aliasing={{1}: (10, {})} | custom-call | flops 671088640 | bytes 8388608 | tf_op jit(solution)/shard_map/pallas_call | solution.py:225
  76.1 4.3 %shard_map.107 = (bf16[512,256]{1,0:T(8,128)(2,1)S(1)}, f32[16,256,128]{2,1,0:T(8,128)S(1)}) custom-call(s32[2]{0:T(128)S(1)} %pad_add_fusion.where_ref, bf16[128,4096]{1,0:T(8,128)(2,1)S(1)} %copy-done.1, bf16[256,2048]{1,0:T(8,128)(2,1)S(1)} %collective-permute-done.1.q_par.refs_1_, ...), custom_call_target="tpu_custom_call", output_to_operand_aliasing={{1}: (10, {})} | custom-call | flops 1342177280 | bytes 8388608 | tf_op jit(solution)/shard_map/pallas_call | solution.py:225
  80.4 9.4 %collective-permute-start.7 = (bf16[528,256]{1,0:T(8,128)(2,1)S(1)}, bf16[528,256]{1,0:T(8,128)(2,1)S(1)}, u32[]{:S(2)}, u32[]{:S(2)}) collective-permute-start(bf16[528,256]{1,0:T(8,128)(2,1)S(1)} %collective-permute-done.5.refs_8_), channel_id=1, source_target_pairs={{0,510},{1,511},{2,0},{3,1},{4,2},{5,3},{6,4},{7,5},{8,6},{9,7},{1... | collective-permute-start | bytes 811016 | tf_op jit(solution)/shard_map/ppermute | solution.py:38
  91.9 4.3 %shard_map.108 = (bf16[512,256]{1,0:T(8,128)(2,1)S(1)}, f32[16,256,128]{2,1,0:T(8,128)S(1)}) custom-call(s32[2]{0:T(128)S(1)} %pad_add_fusion.where_ref, bf16[128,4096]{1,0:T(8,128)(2,1)S(1)} %copy-done.1, bf16[256,2048]{1,0:T(8,128)(2,1)S(1)} %collective-permute-done.1.q_par.refs_1_, ...), custom_call_target="tpu_custom_call", output_to_operand_aliasing={{1}: (10, {})} | custom-call | flops 1342177280 | bytes 8388608 | tf_op jit(solution)/shard_map/pallas_call | solution.py:225
  96.2 4.3 %shard_map.109 = (bf16[512,256]{1,0:T(8,128)(2,1)S(1)}, f32[16,256,128]{2,1,0:T(8,128)S(1)}) custom-call(s32[2]{0:T(128)S(1)} %pad_add_fusion.where_ref, bf16[128,4096]{1,0:T(8,128)(2,1)S(1)} %copy-done.1, bf16[256,2048]{1,0:T(8,128)(2,1)S(1)} %collective-permute-done.1.q_par.refs_1_, ...), custom_call_target="tpu_custom_call", output_to_operand_aliasing={{1}: (10, {})} | custom-call | flops 1342177280 | bytes 8388608 | tf_op jit(solution)/shard_map/pallas_call | solution.py:225
  103.3 6.6 %collective-permute-start.9 = (bf16[528,256]{1,0:T(8,128)(2,1)S(1)}, bf16[528,256]{1,0:T(8,128)(2,1)S(1)}, u32[]{:S(2)}, u32[]{:S(2)}) collective-permute-start(bf16[528,256]{1,0:T(8,128)(2,1)S(1)} %collective-permute-done.7.refs_8_), channel_id=1, source_target_pairs={{0,510},{1,511},{2,0},{3,1},{4,2},{5,3},{6,4},{7,5},{8,6},{9,7},{1... | collective-permute-start | bytes 811016 | tf_op jit(solution)/shard_map/ppermute | solution.py:38
  110.0 4.3 %shard_map.110 = (bf16[512,256]{1,0:T(8,128)(2,1)S(1)}, f32[16,256,128]{2,1,0:T(8,128)S(1)}) custom-call(s32[2]{0:T(128)S(1)} %pad_add_fusion.where_ref, bf16[128,4096]{1,0:T(8,128)(2,1)S(1)} %copy-done.1, bf16[256,2048]{1,0:T(8,128)(2,1)S(1)} %collective-permute-done.1.q_par.refs_1_, ...), custom_call_target="tpu_custom_call", output_to_operand_aliasing={{1}: (10, {})} | custom-call | flops 1342177280 | bytes 8388608 | tf_op jit(solution)/shard_map/pallas_call | solution.py:225
  114.3 4.3 %shard_map.111 = (bf16[512,256]{1,0:T(8,128)(2,1)S(1)}, f32[16,256,128]{2,1,0:T(8,128)S(1)}) custom-call(s32[2]{0:T(128)S(1)} %pad_add_fusion.where_ref, bf16[128,4096]{1,0:T(8,128)(2,1)S(1)} %copy-done.1, bf16[256,2048]{1,0:T(8,128)(2,1)S(1)} %collective-permute-done.1.q_par.refs_1_, ...), custom_call_target="tpu_custom_call", output_to_operand_aliasing={{1}: (10, {})} | custom-call | flops 1342177280 | bytes 8388608 | tf_op jit(solution)/shard_map/pallas_call | solution.py:225
  120.6 4.3 %shard_map.112 = (bf16[512,256]{1,0:T(8,128)(2,1)S(1)}, bf16[128,2048]{1,0:T(8,128)(2,1)S(1)}, bf16[128,2048]{1,0:T(8,128)(2,1)S(1)}) custom-call(s32[2]{0:T(128)S(1)} %pad_add_fusion.where_ref, bf16[128,4096]{1,0:T(8,128)(2,1)S(1)} %copy-done.1, bf16[256,2048]{1,0:T(8,128)(2,1)S(1)} %collective-permute-done.1.q_par.refs_1_, bf16[128,4096]{1,0:T(8,128)(2,1)S(1)} %copy-done, ...), custom_call_target="tpu_custom_call" | custom-call | flops 1342177280 | bytes 8388608 | tf_op jit(solution)/shard_map/pallas_call | solution.py:225
  124.9 3.9 %collective-permute-start.13 = (bf16[512,256]{1,0:T(8,128)(2,1)S(1)}, bf16[512,256]{1,0:T(8,128)(2,1)S(1)}, u32[]{:S(2)}, u32[]{:S(2)}) collective-permute-start(bf16[512,256]{1,0:T(8,128)(2,1)S(1)} %get-tuple-element.88), channel_id=1, source_target_pairs={{0,2},{1,3},{2,4},{3,5},{4,6},{5,7},{6,8},{7,9},{8,10},{9,11},{10,... | collective-permute-start | bytes 786440 | tf_op jit(solution)/shard_map/ppermute | solution.py:38
  128.9 7.4 %collective-permute-start.16 = (bf16[512,256]{1,0:T(8,128)(2,1)S(1)}, bf16[512,256]{1,0:T(8,128)(2,1)S(1)}, u32[]{:S(2)}, u32[]{:S(2)}) collective-permute-start(bf16[512,256]{1,0:T(8,128)(2,1)S(1)} %add_convert_fusion.4), channel_id=1, source_target_pairs={{0,510},{1,511},{2,0},{3,1},{4,2},{5,3},{6,4},{7,5},{8,6},{9,7},{1... | collective-permute-start | bytes 786440 | tf_op jit(solution)/shard_map/ppermute | solution.py:38
  140.4 9.5 %collective-permute-start.17 = (bf16[512,256]{1,0:T(8,128)(2,1)S(1)}, bf16[512,256]{1,0:T(8,128)(2,1)S(1)}, u32[]{:S(2)}, u32[]{:S(2)}) collective-permute-start(bf16[512,256]{1,0:T(8,128)(2,1)S(1)} %add_convert_fusion.3), channel_id=1, source_target_pairs={{0,510},{1,511},{2,0},{3,1},{4,2},{5,3},{6,4},{7,5},{8,6},{9,7},{1... | collective-permute-start | bytes 786440 | tf_op jit(solution)/shard_map/ppermute | solution.py:38
  153.9 3.2 %collective-permute-start.12 = (bf16[128,2048]{1,0:T(8,128)(2,1)S(1)}, bf16[128,2048]{1,0:T(8,128)(2,1)S(1)}, u32[]{:S(2)}, u32[]{:S(2)}) collective-permute-start(bf16[128,2048]{1,0:T(8,128)(2,1)S(1)} %get-tuple-element.87), channel_id=1, source_target_pairs={{0,1},{1,0},{2,3},{3,2},{4,5},{5,4},{6,7},{7,6},{8,9},{9,8},{10,11... | collective-permute-start | bytes 1572872 | tf_op jit(solution)/shard_map/ppermute | solution.py:43
  157.1 15.1 %collective-permute-done.15 = bf16[512,256]{1,0:T(8,128)(2,1)S(1)} collective-permute-done((bf16[512,256]{1,0:T(8,128)(2,1)S(1)}, bf16[512,256]{1,0:T(8,128)(2,1)S(1)}, u32[]{:S(2)}, u32[]{:S(2)}) %collective-permute-start.15) | collective-permute-done | bytes 262176 | tf_op jit(solution)/shard_map/ppermute | solution.py:38
  176.4 6.4 %collective-permute-done.18 = bf16[512,256]{1,0:T(8,128)(2,1)S(1)} collective-permute-done((bf16[512,256]{1,0:T(8,128)(2,1)S(1)}, bf16[512,256]{1,0:T(8,128)(2,1)S(1)}, u32[]{:S(2)}, u32[]{:S(2)}) %collective-permute-start.18) | collective-permute-done | bytes 262176 | tf_op jit(solution)/shard_map/ppermute | solution.py:38
  182.8 10.0 %collective-permute-done.19 = bf16[512,256]{1,0:T(8,128)(2,1)S(1)} collective-permute-done((bf16[512,256]{1,0:T(8,128)(2,1)S(1)}, bf16[512,256]{1,0:T(8,128)(2,1)S(1)}, u32[]{:S(2)}, u32[]{:S(2)}) %collective-permute-start.19) | collective-permute-done | bytes 262176 | tf_op jit(solution)/shard_map/ppermute | solution.py:38
  193.0 3.5 %collective-permute-start.20 = (bf16[256,256]{1,0:T(8,128)(2,1)S(1)}, bf16[256,256]{1,0:T(8,128)(2,1)S(1)}, u32[]{:S(2)}, u32[]{:S(2)}) collective-permute-start(bf16[256,256]{1,0:T(8,128)(2,1)S(1)} %broadcast_select_fusion.5), channel_id=1, source_target_pairs={{0,1},{1,0},{2,3},{3,2},{4,5},{5,4},{6,7},{7,6},{8,9},{9,8},{10,11... | collective-permute-start | bytes 393224 | tf_op jit(solution)/shard_map/ppermute | solution.py:43
  (68 shorter events, 41.0 us)
Async XLA Ops:
  0.6 17.0 %copy-start = (bf16[128,4096]{1,0:T(8,128)(2,1)S(1)}, bf16[128,4096]{1,0:T(8,128)(2,1)}, u32[]{:S(2)}) copy-start(bf16[128,4096]{1,0:T(8,128)(2,1)} %refs_2_.15) | copy-start | bytes 3145732
  0.6 17.0 %copy-start.1 = (bf16[128,4096]{1,0:T(8,128)(2,1)S(1)}, bf16[128,4096]{1,0:T(8,128)(2,1)}, u32[]{:S(2)}) copy-start(bf16[128,4096]{1,0:T(8,128)(2,1)} %refs_0_.15) | copy-start | bytes 3145732
  3.1 20.6 %collective-permute-start.2 = (bf16[272,256]{1,0:T(8,128)(2,1)}, bf16[272,256]{1,0:T(8,128)(2,1)S(1)}, u32[]{:S(2)}, u32[]{:S(2)}) collective-permute-start(bf16[272,256]{1,0:T(8,128)(2,1)} %pad_maximum_fusion.4), channel_id=1, source_target_pairs={{0,1},{1,0},{2,3},{3,2},{4,5},{5,4},{6,7},{7,6},{8,9},{9,8},{10,11... | collective-permute-start | bytes 417800 | tf_op jit(solution)/shard_map/ppermute | solution.py:43
  15.7 6.2 %collective-permute-start = (f32[40,128]{1,0:T(8,128)}, f32[40,128]{1,0:T(8,128)S(1)}, u32[]{:S(2)}, u32[]{:S(2)}) collective-permute-start(f32[40,128]{1,0:T(8,128)} %get-tuple-element.52), channel_id=1, source_target_pairs={{0,1},{1,0},{2,3},{3,2},{4,5},{5,4},{6,7},{7,6},{8,9},{9,8},{10,11... | collective-permute-start | bytes 61448 | tf_op jit(solution)/shard_map/ppermute | solution.py:43
  17.8 24.3 %copy-start.2 = (f32[40,128]{1,0:T(8,128)S(1)}, f32[40,128]{1,0:T(8,128)}, u32[]{:S(2)}) copy-start(f32[40,128]{1,0:T(8,128)} %get-tuple-element.54.sm_own.refs_3_) | copy-start | bytes 61444
  21.9 20.2 %collective-permute-start.1 = (bf16[256,2048]{1,0:T(8,128)(2,1)}, bf16[256,2048]{1,0:T(8,128)(2,1)S(1)}, u32[]{:S(2)}, u32[]{:S(2)}) collective-permute-start(bf16[256,2048]{1,0:T(8,128)(2,1)} %pad_maximum_fusion), channel_id=1, source_target_pairs={{0,1},{1,0},{2,3},{3,2},{4,5},{5,4},{6,7},{7,6},{8,9},{9,8},{10,11... | collective-permute-start | bytes 3145736 | tf_op jit(solution)/shard_map/ppermute | solution.py:43
  23.9 14.5 %collective-permute-start.4 = (bf16[528,256]{1,0:T(8,128)(2,1)S(1)}, bf16[528,256]{1,0:T(8,128)(2,1)S(1)}, u32[]{:S(2)}, u32[]{:S(2)}) collective-permute-start(bf16[528,256]{1,0:T(8,128)(2,1)S(1)} %pad_maximum_fusion.2.refs_8_), channel_id=1, source_target_pairs={{0,2},{1,3},{2,4},{3,5},{4,6},{5,7},{6,8},{7,9},{8,10},{9,11},{10,... | collective-permute-start | bytes 811016 | tf_op jit(solution)/shard_map/ppermute | solution.py:38
  25.9 35.3 %collective-permute-start.3 = (bf16[528,256]{1,0:T(8,128)(2,1)S(1)}, bf16[528,256]{1,0:T(8,128)(2,1)S(1)}, u32[]{:S(2)}, u32[]{:S(2)}) collective-permute-start(bf16[528,256]{1,0:T(8,128)(2,1)S(1)} %pad_maximum_fusion.2.refs_8_), channel_id=1, source_target_pairs={{0,16},{1,17},{2,18},{3,19},{4,20},{5,21},{6,22},{7,23},{8,24},{9,... | collective-permute-start | bytes 811016 | tf_op jit(solution)/shard_map/ppermute | solution.py:38
  38.4 32.5 %collective-permute-start.6 = (bf16[528,256]{1,0:T(8,128)(2,1)S(1)}, bf16[528,256]{1,0:T(8,128)(2,1)S(1)}, u32[]{:S(2)}, u32[]{:S(2)}) collective-permute-start(bf16[528,256]{1,0:T(8,128)(2,1)S(1)} %collective-permute-done.4.refs_9_), channel_id=1, source_target_pairs={{0,2},{1,3},{2,4},{3,5},{4,6},{5,7},{6,8},{7,9},{8,10},{9,11},{10,... | collective-permute-start | bytes 811016 | tf_op jit(solution)/shard_map/ppermute | solution.py:38
  61.2 19.2 %collective-permute-start.5 = (bf16[528,256]{1,0:T(8,128)(2,1)S(1)}, bf16[528,256]{1,0:T(8,128)(2,1)S(1)}, u32[]{:S(2)}, u32[]{:S(2)}) collective-permute-start(bf16[528,256]{1,0:T(8,128)(2,1)S(1)} %collective-permute-done.3), channel_id=1, source_target_pairs={{0,510},{1,511},{2,0},{3,1},{4,2},{5,3},{6,4},{7,5},{8,6},{9,7},{1... | collective-permute-start | bytes 811016 | tf_op jit(solution)/shard_map/ppermute | solution.py:38
  71.0 18.9 %collective-permute-start.8 = (bf16[528,256]{1,0:T(8,128)(2,1)S(1)}, bf16[528,256]{1,0:T(8,128)(2,1)S(1)}, u32[]{:S(2)}, u32[]{:S(2)}) collective-permute-start(bf16[528,256]{1,0:T(8,128)(2,1)S(1)} %collective-permute-done.6.refs_8_), channel_id=1, source_target_pairs={{0,2},{1,3},{2,4},{3,5},{4,6},{5,7},{6,8},{7,9},{8,10},{9,11},{10,... | collective-permute-start | bytes 811016 | tf_op jit(solution)/shard_map/ppermute | solution.py:38
  80.4 20.2 %collective-permute-start.7 = (bf16[528,256]{1,0:T(8,128)(2,1)S(1)}, bf16[528,256]{1,0:T(8,128)(2,1)S(1)}, u32[]{:S(2)}, u32[]{:S(2)}) collective-permute-start(bf16[528,256]{1,0:T(8,128)(2,1)S(1)} %collective-permute-done.5.refs_8_), channel_id=1, source_target_pairs={{0,510},{1,511},{2,0},{3,1},{4,2},{5,3},{6,4},{7,5},{8,6},{9,7},{1... | collective-permute-start | bytes 811016 | tf_op jit(solution)/shard_map/ppermute | solution.py:38
  89.8 13.5 %collective-permute-start.10 = (bf16[528,256]{1,0:T(8,128)(2,1)S(1)}, bf16[528,256]{1,0:T(8,128)(2,1)S(1)}, u32[]{:S(2)}, u32[]{:S(2)}) collective-permute-start(bf16[528,256]{1,0:T(8,128)(2,1)S(1)} %collective-permute-done.8.refs_8_), channel_id=1, source_target_pairs={{0,2},{1,3},{2,4},{3,5},{4,6},{5,7},{6,8},{7,9},{8,10},{9,11},{10,... | collective-permute-start | bytes 811016 | tf_op jit(solution)/shard_map/ppermute | solution.py:38
  103.3 17.3 %collective-permute-start.9 = (bf16[528,256]{1,0:T(8,128)(2,1)S(1)}, bf16[528,256]{1,0:T(8,128)(2,1)S(1)}, u32[]{:S(2)}, u32[]{:S(2)}) collective-permute-start(bf16[528,256]{1,0:T(8,128)(2,1)S(1)} %collective-permute-done.7.refs_8_), channel_id=1, source_target_pairs={{0,510},{1,511},{2,0},{3,1},{4,2},{5,3},{6,4},{7,5},{8,6},{9,7},{1... | collective-permute-start | bytes 811016 | tf_op jit(solution)/shard_map/ppermute | solution.py:38
  118.6 10.2 %collective-permute-start.11 = (bf16[512,256]{1,0:T(8,128)(2,1)S(1)}, bf16[512,256]{1,0:T(8,128)(2,1)S(1)}, u32[]{:S(2)}, u32[]{:S(2)}) collective-permute-start(bf16[512,256]{1,0:T(8,128)(2,1)S(1)} %get-tuple-element.85), channel_id=1, source_target_pairs={{0,510},{1,511},{2,0},{3,1},{4,2},{5,3},{6,4},{7,5},{8,6},{9,7},{1... | collective-permute-start | bytes 786440 | tf_op jit(solution)/shard_map/ppermute | solution.py:38
  124.9 13.4 %collective-permute-start.13 = (bf16[512,256]{1,0:T(8,128)(2,1)S(1)}, bf16[512,256]{1,0:T(8,128)(2,1)S(1)}, u32[]{:S(2)}, u32[]{:S(2)}) collective-permute-start(bf16[512,256]{1,0:T(8,128)(2,1)S(1)} %get-tuple-element.88), channel_id=1, source_target_pairs={{0,2},{1,3},{2,4},{3,5},{4,6},{5,7},{6,8},{7,9},{8,10},{9,11},{10,... | collective-permute-start | bytes 786440 | tf_op jit(solution)/shard_map/ppermute | solution.py:38
  128.9 11.4 %collective-permute-start.16 = (bf16[512,256]{1,0:T(8,128)(2,1)S(1)}, bf16[512,256]{1,0:T(8,128)(2,1)S(1)}, u32[]{:S(2)}, u32[]{:S(2)}) collective-permute-start(bf16[512,256]{1,0:T(8,128)(2,1)S(1)} %add_convert_fusion.4), channel_id=1, source_target_pairs={{0,510},{1,511},{2,0},{3,1},{4,2},{5,3},{6,4},{7,5},{8,6},{9,7},{1... | collective-permute-start | bytes 786440 | tf_op jit(solution)/shard_map/ppermute | solution.py:38
  138.4 13.5 %collective-permute-start.14 = (bf16[512,256]{1,0:T(8,128)(2,1)S(1)}, bf16[512,256]{1,0:T(8,128)(2,1)S(1)}, u32[]{:S(2)}, u32[]{:S(2)}) collective-permute-start(bf16[512,256]{1,0:T(8,128)(2,1)S(1)} %add_convert_fusion.6), channel_id=1, source_target_pairs={{0,2},{1,3},{2,4},{3,5},{4,6},{5,7},{6,8},{7,9},{8,10},{9,11},{10,... | collective-permute-start | bytes 786440 | tf_op jit(solution)/shard_map/ppermute | solution.py:38
  140.4 16.7 %collective-permute-start.17 = (bf16[512,256]{1,0:T(8,128)(2,1)S(1)}, bf16[512,256]{1,0:T(8,128)(2,1)S(1)}, u32[]{:S(2)}, u32[]{:S(2)}) collective-permute-start(bf16[512,256]{1,0:T(8,128)(2,1)S(1)} %add_convert_fusion.3), channel_id=1, source_target_pairs={{0,510},{1,511},{2,0},{3,1},{4,2},{5,3},{6,4},{7,5},{8,6},{9,7},{1... | collective-permute-start | bytes 786440 | tf_op jit(solution)/shard_map/ppermute | solution.py:38
  152.0 20.2 %collective-permute-start.15 = (bf16[512,256]{1,0:T(8,128)(2,1)S(1)}, bf16[512,256]{1,0:T(8,128)(2,1)S(1)}, u32[]{:S(2)}, u32[]{:S(2)}) collective-permute-start(bf16[512,256]{1,0:T(8,128)(2,1)S(1)} %add_convert_fusion.5), channel_id=1, source_target_pairs={{0,2},{1,3},{2,4},{3,5},{4,6},{5,7},{6,8},{7,9},{8,10},{9,11},{10,... | collective-permute-start | bytes 786440 | tf_op jit(solution)/shard_map/ppermute | solution.py:38
  153.9 22.4 %collective-permute-start.12 = (bf16[128,2048]{1,0:T(8,128)(2,1)S(1)}, bf16[128,2048]{1,0:T(8,128)(2,1)S(1)}, u32[]{:S(2)}, u32[]{:S(2)}) collective-permute-start(bf16[128,2048]{1,0:T(8,128)(2,1)S(1)} %get-tuple-element.87), channel_id=1, source_target_pairs={{0,1},{1,0},{2,3},{3,2},{4,5},{5,4},{6,7},{7,6},{8,9},{9,8},{10,11... | collective-permute-start | bytes 1572872 | tf_op jit(solution)/shard_map/ppermute | solution.py:43
  172.3 10.5 %collective-permute-start.18 = (bf16[512,256]{1,0:T(8,128)(2,1)S(1)}, bf16[512,256]{1,0:T(8,128)(2,1)S(1)}, u32[]{:S(2)}, u32[]{:S(2)}) collective-permute-start(bf16[512,256]{1,0:T(8,128)(2,1)S(1)} %add_convert_fusion.2), channel_id=1, source_target_pairs={{0,510},{1,511},{2,0},{3,1},{4,2},{5,3},{6,4},{7,5},{8,6},{9,7},{1... | collective-permute-start | bytes 786440 | tf_op jit(solution)/shard_map/ppermute | solution.py:38
  174.4 18.5 %collective-permute-start.19 = (bf16[512,256]{1,0:T(8,128)(2,1)S(1)}, bf16[512,256]{1,0:T(8,128)(2,1)S(1)}, u32[]{:S(2)}, u32[]{:S(2)}) collective-permute-start(bf16[512,256]{1,0:T(8,128)(2,1)S(1)} %add_convert_fusion.1), channel_id=1, source_target_pairs={{0,496},{1,497},{2,498},{3,499},{4,500},{5,501},{6,502},{7,503},{8... | collective-permute-start | bytes 786440 | tf_op jit(solution)/shard_map/ppermute | solution.py:38
  193.0 6.9 %collective-permute-start.20 = (bf16[256,256]{1,0:T(8,128)(2,1)S(1)}, bf16[256,256]{1,0:T(8,128)(2,1)S(1)}, u32[]{:S(2)}, u32[]{:S(2)}) collective-permute-start(bf16[256,256]{1,0:T(8,128)(2,1)S(1)} %broadcast_select_fusion.5), channel_id=1, source_target_pairs={{0,1},{1,0},{2,3},{3,2},{4,5},{5,4},{6,7},{7,6},{8,9},{9,8},{10,11... | collective-permute-start | bytes 393224 | tf_op jit(solution)/shard_map/ppermute | solution.py:43

commit v3 on v2

--- a/solution.py
+++ b/solution.py
@@ -374,19 +374,16 @@
     blocks[7] = shift(blocks[8], -2)
     blocks[2], blocks[8] = tie(blocks[2], blocks[8])
     blocks[3] = shift(blocks[2], 2)
-    work((8,))
-    work((2,))
+    work((8, 2))
     blocks[7] = then(blocks[7])
     blocks[3] = then(blocks[3])
     blocks[6] = shift(blocks[7], -2)
     blocks[4] = shift(blocks[3], 2)
-    work((7,))
-    work((3,))
+    work((7, 3))
     blocks[6] = then(blocks[6])
     blocks[4] = then(blocks[4])
     blocks[5] = shift(blocks[6], -2)
-    work((6,))
-    work((4,))
+    work((6, 4))
     near = shift(parts[4], -2)
     blocks[5] = then(blocks[5])
     work((5,), True)

time: 202 us -> 196 us (0.970)
  the two profiles are of different devices: /device:TPU:2 before, /device:TPU:32 now
where the time goes in v3:
time: 196 us
  starting transfers between devices  106 us (54%)
  waiting for transfers between devices  46.9 us (24%)
  Pallas kernels  33.6 us (17%)
  other arithmetic  6.3 us (3%)
    ppermute x16, starting transfers between devices, shift(): lax.ppermute(array, AXES, [(i, (i + by) % count) for i in range(count)])  92.5 us
    ppermute x16, waiting for transfers between devices, shift(): lax.ppermute(array, AXES, [(i, (i + by) % count) for i in range(count)])  38.9 us
    pallas_call x5, Pallas kernels, pair_grads(): pl.pallas_call(functools.partial(pair_kernel, offsets, first, last), in_s...  29.5 us
    ppermute x5, starting transfers between devices, swap(): return lax.ppermute(array, AXES, [(i, i ^ 1) for i in range(count)])  13.1 us
    ppermute x5, waiting for transfers between devices, swap(): return lax.ppermute(array, AXES, [(i, i ^ 1) for i in range(count)])  8.02 us
  transfers between devices with their start and end apart: 21, of which 10 were waited for; matrix products, arithmetic and copies ran while one was open for 2% of the time, Pallas kernels for 17%

profile of v3, /device:TPU:32, one launch (start us, length us, event | category | flops | bytes accessed | tf_op | source)
XLA Modules:
  0.0 195.6 jit_solution(1827107856630779744)
XLA Ops:
  3.1 3.4 %collective-permute-start.2 = (bf16[272,256]{1,0:T(8,128)(2,1)}, bf16[272,256]{1,0:T(8,128)(2,1)S(1)}, u32[]{:S(2)}, u32[]{:S(2)}) collective-permute-start(bf16[272,256]{1,0:T(8,128)(2,1)} %pad_maximum_fusion.4), channel_id=1, source_target_pairs={{0,1},{1,0},{2,3},{3,2},{4,5},{5,4},{6,7},{7,6},{8,9},{9,8},{10,11... | collective-permute-start | bytes 417800 | tf_op jit(solution)/shard_map/ppermute | solution.py:43
  8.0 3.3 %shard_map.103 = (f32[40,128]{1,0:T(8,128)}, f32[40,128]{1,0:T(8,128)}) custom-call(s32[1]{0:T(128)} %bitcast.column_ref, bf16[128,4096]{1,0:T(8,128)(2,1)} %out_ref.1, bf16[128,4096]{1,0:T(8,128)(2,1)} %refs_2_.9, f32[32,128]{1,0:T(8,128)} %lse_ref, f32[8,128]{1,0:T(8,128)} %maximum_maximum_fusion.tail_ref), custom_call_target="tpu_custom_call" | custom-call | flops 16777216 | bytes 2097152 | tf_op jit(solution)/shard_map/pallas_call | solution.py:288
  19.8 3.8 %collective-permute-start.4 = (bf16[528,256]{1,0:T(8,128)(2,1)S(1)}, bf16[528,256]{1,0:T(8,128)(2,1)S(1)}, u32[]{:S(2)}, u32[]{:S(2)}) collective-permute-start(bf16[528,256]{1,0:T(8,128)(2,1)S(1)} %pad_maximum_fusion.2.refs_8_), channel_id=1, source_target_pairs={{0,2},{1,3},{2,4},{3,5},{4,6},{5,7},{6,8},{7,9},{8,10},{9,11},{10,... | collective-permute-start | bytes 811016 | tf_op jit(solution)/shard_map/ppermute | solution.py:38
  23.6 13.9 %collective-permute-start.3 = (bf16[528,256]{1,0:T(8,128)(2,1)S(1)}, bf16[528,256]{1,0:T(8,128)(2,1)S(1)}, u32[]{:S(2)}, u32[]{:S(2)}) collective-permute-start(bf16[528,256]{1,0:T(8,128)(2,1)S(1)} %pad_maximum_fusion.2.refs_8_), channel_id=1, source_target_pairs={{0,16},{1,17},{2,18},{3,19},{4,20},{5,21},{6,22},{7,23},{8,24},{9,... | collective-permute-start | bytes 811016 | tf_op jit(solution)/shard_map/ppermute | solution.py:38
  37.5 2.9 %collective-permute-start.6 = (bf16[528,256]{1,0:T(8,128)(2,1)S(1)}, bf16[528,256]{1,0:T(8,128)(2,1)S(1)}, u32[]{:S(2)}, u32[]{:S(2)}) collective-permute-start(bf16[528,256]{1,0:T(8,128)(2,1)S(1)} %collective-permute-done.4.refs_9_), channel_id=1, source_target_pairs={{0,2},{1,3},{2,4},{3,5},{4,6},{5,7},{6,8},{7,9},{8,10},{9,11},{10,... | collective-permute-start | bytes 811016 | tf_op jit(solution)/shard_map/ppermute | solution.py:38
  43.5 7.6 %shard_map.105 = (bf16[512,256]{1,0:T(8,128)(2,1)S(1)}, bf16[512,256]{1,0:T(8,128)(2,1)S(1)}, f32[16,256,128]{2,1,0:T(8,128)S(1)}) custom-call(s32[2]{0:T(128)S(1)} %pad_add_fusion.where_ref, bf16[128,4096]{1,0:T(8,128)(2,1)S(1)} %copy-done.1, bf16[256,2048]{1,0:T(8,128)(2,1)S(1)} %collective-permute-done.1.q_par.refs_1_, bf16[128,4096]{1,0:T(8,128)(2,1)S(1)} %copy-done, ...), custom_call_target="tpu_custom_call" | custom-call | flops 2684354560 | bytes 8388608 | tf_op jit(solution)/shard_map/pallas_call | solution.py:225
  51.9 14.1 %collective-permute-start.5 = (bf16[528,256]{1,0:T(8,128)(2,1)S(1)}, bf16[528,256]{1,0:T(8,128)(2,1)S(1)}, u32[]{:S(2)}, u32[]{:S(2)}) collective-permute-start(bf16[528,256]{1,0:T(8,128)(2,1)S(1)} %collective-permute-done.3), channel_id=1, source_target_pairs={{0,510},{1,511},{2,0},{3,1},{4,2},{5,3},{6,4},{7,5},{8,6},{9,7},{1... | collective-permute-start | bytes 811016 | tf_op jit(solution)/shard_map/ppermute | solution.py:38
  66.1 3.2 %collective-permute-start.8 = (bf16[528,256]{1,0:T(8,128)(2,1)S(1)}, bf16[528,256]{1,0:T(8,128)(2,1)S(1)}, u32[]{:S(2)}, u32[]{:S(2)}) collective-permute-start(bf16[528,256]{1,0:T(8,128)(2,1)S(1)} %collective-permute-done.6.refs_9_), channel_id=1, source_target_pairs={{0,2},{1,3},{2,4},{3,5},{4,6},{5,7},{6,8},{7,9},{8,10},{9,11},{10,... | collective-permute-start | bytes 811016 | tf_op jit(solution)/shard_map/ppermute | solution.py:38
  69.3 5.6 %shard_map.106 = (bf16[256,256]{1,0:T(8,128)(2,1)S(1)}, bf16[512,256]{1,0:T(8,128)(2,1)S(1)}, f32[16,256,128]{2,1,0:T(8,128)S(1)}) custom-call(s32[2]{0:T(128)S(1)} %pad_add_fusion.where_ref, bf16[128,4096]{1,0:T(8,128)(2,1)S(1)} %copy-done.1, bf16[256,2048]{1,0:T(8,128)(2,1)S(1)} %collective-permute-done.1.q_par.refs_1_, ...), custom_call_target="tpu_custom_call", output_to_operand_aliasing={{2}: (11, {})} | custom-call | flops 2013265920 | bytes 8388608 | tf_op jit(solution)/shard_map/pallas_call | solution.py:225
  74.9 6.3 %collective-permute-start.7 = (bf16[528,256]{1,0:T(8,128)(2,1)S(1)}, bf16[528,256]{1,0:T(8,128)(2,1)S(1)}, u32[]{:S(2)}, u32[]{:S(2)}) collective-permute-start(bf16[528,256]{1,0:T(8,128)(2,1)S(1)} %collective-permute-done.5.refs_8_), channel_id=1, source_target_pairs={{0,510},{1,511},{2,0},{3,1},{4,2},{5,3},{6,4},{7,5},{8,6},{9,7},{1... | collective-permute-start | bytes 811016 | tf_op jit(solution)/shard_map/ppermute | solution.py:38
  83.2 6.0 %shard_map.107 = (bf16[512,256]{1,0:T(8,128)(2,1)S(1)}, bf16[512,256]{1,0:T(8,128)(2,1)S(1)}, f32[16,256,128]{2,1,0:T(8,128)S(1)}) custom-call(s32[2]{0:T(128)S(1)} %pad_add_fusion.where_ref, bf16[128,4096]{1,0:T(8,128)(2,1)S(1)} %copy-done.1, bf16[256,2048]{1,0:T(8,128)(2,1)S(1)} %collective-permute-done.1.q_par.refs_1_, ...), custom_call_target="tpu_custom_call", output_to_operand_aliasing={{2}: (11, {})} | custom-call | flops 2684354560 | bytes 8388608 | tf_op jit(solution)/shard_map/pallas_call | solution.py:225
  89.2 5.8 %collective-permute-done.10.refs_9_ = bf16[528,256]{1,0:T(8,128)(2,1)S(1)} collective-permute-done((bf16[528,256]{1,0:T(8,128)(2,1)S(1)}, bf16[528,256]{1,0:T(8,128)(2,1)S(1)}, u32[]{:S(2)}, u32[]{:S(2)}) %collective-permute-start.10) | collective-permute-done | bytes 270368 | tf_op jit(solution)/shard_map/ppermute | solution.py:38
  95.1 9.2 %collective-permute-start.9 = (bf16[528,256]{1,0:T(8,128)(2,1)S(1)}, bf16[528,256]{1,0:T(8,128)(2,1)S(1)}, u32[]{:S(2)}, u32[]{:S(2)}) collective-permute-start(bf16[528,256]{1,0:T(8,128)(2,1)S(1)} %collective-permute-done.7.refs_8_), channel_id=1, source_target_pairs={{0,510},{1,511},{2,0},{3,1},{4,2},{5,3},{6,4},{7,5},{8,6},{9,7},{1... | collective-permute-start | bytes 811016 | tf_op jit(solution)/shard_map/ppermute | solution.py:38
  104.3 6.0 %shard_map.108 = (bf16[512,256]{1,0:T(8,128)(2,1)S(1)}, bf16[512,256]{1,0:T(8,128)(2,1)S(1)}, f32[16,256,128]{2,1,0:T(8,128)S(1)}) custom-call(s32[2]{0:T(128)S(1)} %pad_add_fusion.where_ref, bf16[128,4096]{1,0:T(8,128)(2,1)S(1)} %copy-done.1, bf16[256,2048]{1,0:T(8,128)(2,1)S(1)} %collective-permute-done.1.q_par.refs_1_, ...), custom_call_target="tpu_custom_call", output_to_operand_aliasing={{2}: (11, {})} | custom-call | flops 2684354560 | bytes 8388608 | tf_op jit(solution)/shard_map/pallas_call | solution.py:225
  110.3 3.8 %collective-permute-start.11 = (bf16[512,256]{1,0:T(8,128)(2,1)S(1)}, bf16[512,256]{1,0:T(8,128)(2,1)S(1)}, u32[]{:S(2)}, u32[]{:S(2)}) collective-permute-start(bf16[512,256]{1,0:T(8,128)(2,1)S(1)} %get-tuple-element.79), channel_id=1, source_target_pairs={{0,510},{1,511},{2,0},{3,1},{4,2},{5,3},{6,4},{7,5},{8,6},{9,7},{1... | collective-permute-start | bytes 786440 | tf_op jit(solution)/shard_map/ppermute | solution.py:38
  114.2 4.3 %shard_map.109 = (bf16[512,256]{1,0:T(8,128)(2,1)S(1)}, bf16[128,2048]{1,0:T(8,128)(2,1)S(1)}, bf16[128,2048]{1,0:T(8,128)(2,1)S(1)}) custom-call(s32[2]{0:T(128)S(1)} %pad_add_fusion.where_ref, bf16[128,4096]{1,0:T(8,128)(2,1)S(1)} %copy-done.1, bf16[256,2048]{1,0:T(8,128)(2,1)S(1)} %collective-permute-done.1.q_par.refs_1_, bf16[128,4096]{1,0:T(8,128)(2,1)S(1)} %copy-done, ...), custom_call_target="tpu_custom_call" | custom-call | flops 1342177280 | bytes 8388608 | tf_op jit(solution)/shard_map/pallas_call | solution.py:225
  120.6 3.8 %collective-permute-start.16 = (bf16[512,256]{1,0:T(8,128)(2,1)S(1)}, bf16[512,256]{1,0:T(8,128)(2,1)S(1)}, u32[]{:S(2)}, u32[]{:S(2)}) collective-permute-start(bf16[512,256]{1,0:T(8,128)(2,1)S(1)} %add_convert_fusion.4), channel_id=1, source_target_pairs={{0,510},{1,511},{2,0},{3,1},{4,2},{5,3},{6,4},{7,5},{8,6},{9,7},{1... | collective-permute-start | bytes 786440 | tf_op jit(solution)/shard_map/ppermute | solution.py:38
  129.2 6.7 %collective-permute-start.17 = (bf16[512,256]{1,0:T(8,128)(2,1)S(1)}, bf16[512,256]{1,0:T(8,128)(2,1)S(1)}, u32[]{:S(2)}, u32[]{:S(2)}) collective-permute-start(bf16[512,256]{1,0:T(8,128)(2,1)S(1)} %add_convert_fusion.3), channel_id=1, source_target_pairs={{0,510},{1,511},{2,0},{3,1},{4,2},{5,3},{6,4},{7,5},{8,6},{9,7},{1... | collective-permute-start | bytes 786440 | tf_op jit(solution)/shard_map/ppermute | solution.py:38
  140.3 2.7 %collective-permute-start.12 = (bf16[128,2048]{1,0:T(8,128)(2,1)S(1)}, bf16[128,2048]{1,0:T(8,128)(2,1)S(1)}, u32[]{:S(2)}, u32[]{:S(2)}) collective-permute-start(bf16[128,2048]{1,0:T(8,128)(2,1)S(1)} %get-tuple-element.81), channel_id=1, source_target_pairs={{0,1},{1,0},{2,3},{3,2},{4,5},{5,4},{6,7},{7,6},{8,9},{9,8},{10,11... | collective-permute-start | bytes 1572872 | tf_op jit(solution)/shard_map/ppermute | solution.py:43
  143.0 12.6 %collective-permute-done.15 = bf16[512,256]{1,0:T(8,128)(2,1)S(1)} collective-permute-done((bf16[512,256]{1,0:T(8,128)(2,1)S(1)}, bf16[512,256]{1,0:T(8,128)(2,1)S(1)}, u32[]{:S(2)}, u32[]{:S(2)}) %collective-permute-start.15) | collective-permute-done | bytes 262176 | tf_op jit(solution)/shard_map/ppermute | solution.py:38
  155.6 14.5 %collective-permute-start.18 = (bf16[512,256]{1,0:T(8,128)(2,1)S(1)}, bf16[512,256]{1,0:T(8,128)(2,1)S(1)}, u32[]{:S(2)}, u32[]{:S(2)}) collective-permute-start(bf16[512,256]{1,0:T(8,128)(2,1)S(1)} %add_convert_fusion.2), channel_id=1, source_target_pairs={{0,510},{1,511},{2,0},{3,1},{4,2},{5,3},{6,4},{7,5},{8,6},{9,7},{1... | collective-permute-start | bytes 786440 | tf_op jit(solution)/shard_map/ppermute | solution.py:38
  172.2 2.9 %collective-permute-done.18 = bf16[512,256]{1,0:T(8,128)(2,1)S(1)} collective-permute-done((bf16[512,256]{1,0:T(8,128)(2,1)S(1)}, bf16[512,256]{1,0:T(8,128)(2,1)S(1)}, u32[]{:S(2)}, u32[]{:S(2)}) %collective-permute-start.18) | collective-permute-done | bytes 262176 | tf_op jit(solution)/shard_map/ppermute | solution.py:38
  175.2 12.0 %collective-permute-done.19 = bf16[512,256]{1,0:T(8,128)(2,1)S(1)} collective-permute-done((bf16[512,256]{1,0:T(8,128)(2,1)S(1)}, bf16[512,256]{1,0:T(8,128)(2,1)S(1)}, u32[]{:S(2)}, u32[]{:S(2)}) %collective-permute-start.19) | collective-permute-done | bytes 262176 | tf_op jit(solution)/shard_map/ppermute | solution.py:38
  190.6 3.6 %collective-permute-done.20 = bf16[256,256]{1,0:T(8,128)(2,1)S(1)} collective-permute-done((bf16[256,256]{1,0:T(8,128)(2,1)S(1)}, bf16[256,256]{1,0:T(8,128)(2,1)S(1)}, u32[]{:S(2)}, u32[]{:S(2)}) %collective-permute-start.20) | collective-permute-done | bytes 131104 | tf_op jit(solution)/shard_map/ppermute | solution.py:43
  (65 shorter events, 35.4 us)
Async XLA Ops:
  0.6 13.1 %copy-start = (bf16[128,4096]{1,0:T(8,128)(2,1)S(1)}, bf16[128,4096]{1,0:T(8,128)(2,1)}, u32[]{:S(2)}) copy-start(bf16[128,4096]{1,0:T(8,128)(2,1)} %refs_2_.9) | copy-start | bytes 3145732
  0.6 13.1 %copy-start.1 = (bf16[128,4096]{1,0:T(8,128)(2,1)S(1)}, bf16[128,4096]{1,0:T(8,128)(2,1)}, u32[]{:S(2)}) copy-start(bf16[128,4096]{1,0:T(8,128)(2,1)} %refs_0_.9) | copy-start | bytes 3145732
  3.1 16.5 %collective-permute-start.2 = (bf16[272,256]{1,0:T(8,128)(2,1)}, bf16[272,256]{1,0:T(8,128)(2,1)S(1)}, u32[]{:S(2)}, u32[]{:S(2)}) collective-permute-start(bf16[272,256]{1,0:T(8,128)(2,1)} %pad_maximum_fusion.4), channel_id=1, source_target_pairs={{0,1},{1,0},{2,3},{3,2},{4,5},{5,4},{6,7},{7,6},{8,9},{9,8},{10,11... | collective-permute-start | bytes 417800 | tf_op jit(solution)/shard_map/ppermute | solution.py:43
  11.3 5.9 %collective-permute-start = (f32[40,128]{1,0:T(8,128)}, f32[40,128]{1,0:T(8,128)S(1)}, u32[]{:S(2)}, u32[]{:S(2)}) collective-permute-start(f32[40,128]{1,0:T(8,128)} %get-tuple-element.49), channel_id=1, source_target_pairs={{0,1},{1,0},{2,3},{3,2},{4,5},{5,4},{6,7},{7,6},{8,9},{9,8},{10,11... | collective-permute-start | bytes 61448 | tf_op jit(solution)/shard_map/ppermute | solution.py:43
  13.9 28.9 %copy-start.2 = (f32[40,128]{1,0:T(8,128)S(1)}, f32[40,128]{1,0:T(8,128)}, u32[]{:S(2)}) copy-start(f32[40,128]{1,0:T(8,128)} %get-tuple-element.51.sm_own.refs_3_) | copy-start | bytes 61444
  17.2 25.6 %collective-permute-start.1 = (bf16[256,2048]{1,0:T(8,128)(2,1)}, bf16[256,2048]{1,0:T(8,128)(2,1)S(1)}, u32[]{:S(2)}, u32[]{:S(2)}) collective-permute-start(bf16[256,2048]{1,0:T(8,128)(2,1)} %pad_maximum_fusion), channel_id=1, source_target_pairs={{0,1},{1,0},{2,3},{3,2},{4,5},{5,4},{6,7},{7,6},{8,9},{9,8},{10,11... | collective-permute-start | bytes 3145736 | tf_op jit(solution)/shard_map/ppermute | solution.py:43
  19.8 17.8 %collective-permute-start.4 = (bf16[528,256]{1,0:T(8,128)(2,1)S(1)}, bf16[528,256]{1,0:T(8,128)(2,1)S(1)}, u32[]{:S(2)}, u32[]{:S(2)}) collective-permute-start(bf16[528,256]{1,0:T(8,128)(2,1)S(1)} %pad_maximum_fusion.2.refs_8_), channel_id=1, source_target_pairs={{0,2},{1,3},{2,4},{3,5},{4,6},{5,7},{6,8},{7,9},{8,10},{9,11},{10,... | collective-permute-start | bytes 811016 | tf_op jit(solution)/shard_map/ppermute | solution.py:38
  23.6 28.3 %collective-permute-start.3 = (bf16[528,256]{1,0:T(8,128)(2,1)S(1)}, bf16[528,256]{1,0:T(8,128)(2,1)S(1)}, u32[]{:S(2)}, u32[]{:S(2)}) collective-permute-start(bf16[528,256]{1,0:T(8,128)(2,1)S(1)} %pad_maximum_fusion.2.refs_8_), channel_id=1, source_target_pairs={{0,16},{1,17},{2,18},{3,19},{4,20},{5,21},{6,22},{7,23},{8,24},{9,... | collective-permute-start | bytes 811016 | tf_op jit(solution)/shard_map/ppermute | solution.py:38
  37.5 28.5 %collective-permute-start.6 = (bf16[528,256]{1,0:T(8,128)(2,1)S(1)}, bf16[528,256]{1,0:T(8,128)(2,1)S(1)}, u32[]{:S(2)}, u32[]{:S(2)}) collective-permute-start(bf16[528,256]{1,0:T(8,128)(2,1)S(1)} %collective-permute-done.4.refs_9_), channel_id=1, source_target_pairs={{0,2},{1,3},{2,4},{3,5},{4,6},{5,7},{6,8},{7,9},{8,10},{9,11},{10,... | collective-permute-start | bytes 811016 | tf_op jit(solution)/shard_map/ppermute | solution.py:38
  51.9 23.0 %collective-permute-start.5 = (bf16[528,256]{1,0:T(8,128)(2,1)S(1)}, bf16[528,256]{1,0:T(8,128)(2,1)S(1)}, u32[]{:S(2)}, u32[]{:S(2)}) collective-permute-start(bf16[528,256]{1,0:T(8,128)(2,1)S(1)} %collective-permute-done.3), channel_id=1, source_target_pairs={{0,510},{1,511},{2,0},{3,1},{4,2},{5,3},{6,4},{7,5},{8,6},{9,7},{1... | collective-permute-start | bytes 811016 | tf_op jit(solution)/shard_map/ppermute | solution.py:38
  66.1 15.2 %collective-permute-start.8 = (bf16[528,256]{1,0:T(8,128)(2,1)S(1)}, bf16[528,256]{1,0:T(8,128)(2,1)S(1)}, u32[]{:S(2)}, u32[]{:S(2)}) collective-permute-start(bf16[528,256]{1,0:T(8,128)(2,1)S(1)} %collective-permute-done.6.refs_9_), channel_id=1, source_target_pairs={{0,2},{1,3},{2,4},{3,5},{4,6},{5,7},{6,8},{7,9},{8,10},{9,11},{10,... | collective-permute-start | bytes 811016 | tf_op jit(solution)/shard_map/ppermute | solution.py:38
  74.9 14.3 %collective-permute-start.7 = (bf16[528,256]{1,0:T(8,128)(2,1)S(1)}, bf16[528,256]{1,0:T(8,128)(2,1)S(1)}, u32[]{:S(2)}, u32[]{:S(2)}) collective-permute-start(bf16[528,256]{1,0:T(8,128)(2,1)S(1)} %collective-permute-done.5.refs_8_), channel_id=1, source_target_pairs={{0,510},{1,511},{2,0},{3,1},{4,2},{5,3},{6,4},{7,5},{8,6},{9,7},{1... | collective-permute-start | bytes 811016 | tf_op jit(solution)/shard_map/ppermute | solution.py:38
  81.3 13.8 %collective-permute-start.10 = (bf16[528,256]{1,0:T(8,128)(2,1)S(1)}, bf16[528,256]{1,0:T(8,128)(2,1)S(1)}, u32[]{:S(2)}, u32[]{:S(2)}) collective-permute-start(bf16[528,256]{1,0:T(8,128)(2,1)S(1)} %collective-permute-done.8.refs_9_), channel_id=1, source_target_pairs={{0,2},{1,3},{2,4},{3,5},{4,6},{5,7},{6,8},{7,9},{8,10},{9,11},{10,... | collective-permute-start | bytes 811016 | tf_op jit(solution)/shard_map/ppermute | solution.py:38
  95.1 19.1 %collective-permute-start.9 = (bf16[528,256]{1,0:T(8,128)(2,1)S(1)}, bf16[528,256]{1,0:T(8,128)(2,1)S(1)}, u32[]{:S(2)}, u32[]{:S(2)}) collective-permute-start(bf16[528,256]{1,0:T(8,128)(2,1)S(1)} %collective-permute-done.7.refs_8_), channel_id=1, source_target_pairs={{0,510},{1,511},{2,0},{3,1},{4,2},{5,3},{6,4},{7,5},{8,6},{9,7},{1... | collective-permute-start | bytes 811016 | tf_op jit(solution)/shard_map/ppermute | solution.py:38
  110.3 10.2 %collective-permute-start.11 = (bf16[512,256]{1,0:T(8,128)(2,1)S(1)}, bf16[512,256]{1,0:T(8,128)(2,1)S(1)}, u32[]{:S(2)}, u32[]{:S(2)}) collective-permute-start(bf16[512,256]{1,0:T(8,128)(2,1)S(1)} %get-tuple-element.79), channel_id=1, source_target_pairs={{0,510},{1,511},{2,0},{3,1},{4,2},{5,3},{6,4},{7,5},{8,6},{9,7},{1... | collective-permute-start | bytes 786440 | tf_op jit(solution)/shard_map/ppermute | solution.py:38
  118.5 8.3 %collective-permute-start.13 = (bf16[512,256]{1,0:T(8,128)(2,1)S(1)}, bf16[512,256]{1,0:T(8,128)(2,1)S(1)}, u32[]{:S(2)}, u32[]{:S(2)}) collective-permute-start(bf16[512,256]{1,0:T(8,128)(2,1)S(1)} %get-tuple-element.82), channel_id=1, source_target_pairs={{0,2},{1,3},{2,4},{3,5},{4,6},{5,7},{6,8},{7,9},{8,10},{9,11},{10,... | collective-permute-start | bytes 786440 | tf_op jit(solution)/shard_map/ppermute | solution.py:38
  120.6 8.5 %collective-permute-start.16 = (bf16[512,256]{1,0:T(8,128)(2,1)S(1)}, bf16[512,256]{1,0:T(8,128)(2,1)S(1)}, u32[]{:S(2)}, u32[]{:S(2)}) collective-permute-start(bf16[512,256]{1,0:T(8,128)(2,1)S(1)} %add_convert_fusion.4), channel_id=1, source_target_pairs={{0,510},{1,511},{2,0},{3,1},{4,2},{5,3},{6,4},{7,5},{8,6},{9,7},{1... | collective-permute-start | bytes 786440 | tf_op jit(solution)/shard_map/ppermute | solution.py:38
  126.9 11.4 %collective-permute-start.14 = (bf16[512,256]{1,0:T(8,128)(2,1)S(1)}, bf16[512,256]{1,0:T(8,128)(2,1)S(1)}, u32[]{:S(2)}, u32[]{:S(2)}) collective-permute-start(bf16[512,256]{1,0:T(8,128)(2,1)S(1)} %add_convert_fusion.6), channel_id=1, source_target_pairs={{0,2},{1,3},{2,4},{3,5},{4,6},{5,7},{6,8},{7,9},{8,10},{9,11},{10,... | collective-permute-start | bytes 786440 | tf_op jit(solution)/shard_map/ppermute | solution.py:38
  129.2 13.7 %collective-permute-start.17 = (bf16[512,256]{1,0:T(8,128)(2,1)S(1)}, bf16[512,256]{1,0:T(8,128)(2,1)S(1)}, u32[]{:S(2)}, u32[]{:S(2)}) collective-permute-start(bf16[512,256]{1,0:T(8,128)(2,1)S(1)} %add_convert_fusion.3), channel_id=1, source_target_pairs={{0,510},{1,511},{2,0},{3,1},{4,2},{5,3},{6,4},{7,5},{8,6},{9,7},{1... | collective-permute-start | bytes 786440 | tf_op jit(solution)/shard_map/ppermute | solution.py:38
  138.3 17.2 %collective-permute-start.15 = (bf16[512,256]{1,0:T(8,128)(2,1)S(1)}, bf16[512,256]{1,0:T(8,128)(2,1)S(1)}, u32[]{:S(2)}, u32[]{:S(2)}) collective-permute-start(bf16[512,256]{1,0:T(8,128)(2,1)S(1)} %add_convert_fusion.5), channel_id=1, source_target_pairs={{0,2},{1,3},{2,4},{3,5},{4,6},{5,7},{6,8},{7,9},{8,10},{9,11},{10,... | collective-permute-start | bytes 786440 | tf_op jit(solution)/shard_map/ppermute | solution.py:38
  140.3 31.9 %collective-permute-start.12 = (bf16[128,2048]{1,0:T(8,128)(2,1)S(1)}, bf16[128,2048]{1,0:T(8,128)(2,1)S(1)}, u32[]{:S(2)}, u32[]{:S(2)}) collective-permute-start(bf16[128,2048]{1,0:T(8,128)(2,1)S(1)} %get-tuple-element.81), channel_id=1, source_target_pairs={{0,1},{1,0},{2,3},{3,2},{4,5},{5,4},{6,7},{7,6},{8,9},{9,8},{10,11... | collective-permute-start | bytes 1572872 | tf_op jit(solution)/shard_map/ppermute | solution.py:43
  155.6 19.5 %collective-permute-start.18 = (bf16[512,256]{1,0:T(8,128)(2,1)S(1)}, bf16[512,256]{1,0:T(8,128)(2,1)S(1)}, u32[]{:S(2)}, u32[]{:S(2)}) collective-permute-start(bf16[512,256]{1,0:T(8,128)(2,1)S(1)} %add_convert_fusion.2), channel_id=1, source_target_pairs={{0,510},{1,511},{2,0},{3,1},{4,2},{5,3},{6,4},{7,5},{8,6},{9,7},{1... | collective-permute-start | bytes 786440 | tf_op jit(solution)/shard_map/ppermute | solution.py:38
  170.2 17.0 %collective-permute-start.19 = (bf16[512,256]{1,0:T(8,128)(2,1)S(1)}, bf16[512,256]{1,0:T(8,128)(2,1)S(1)}, u32[]{:S(2)}, u32[]{:S(2)}) collective-permute-start(bf16[512,256]{1,0:T(8,128)(2,1)S(1)} %add_convert_fusion.1), channel_id=1, source_target_pairs={{0,496},{1,497},{2,498},{3,499},{4,500},{5,501},{6,502},{7,503},{8... | collective-permute-start | bytes 786440 | tf_op jit(solution)/shard_map/ppermute | solution.py:38
  187.3 6.9 %collective-permute-start.20 = (bf16[256,256]{1,0:T(8,128)(2,1)S(1)}, bf16[256,256]{1,0:T(8,128)(2,1)S(1)}, u32[]{:S(2)}, u32[]{:S(2)}) collective-permute-start(bf16[256,256]{1,0:T(8,128)(2,1)S(1)} %broadcast_select_fusion.5), channel_id=1, source_target_pairs={{0,1},{1,0},{2,3},{3,2},{4,5},{5,4},{6,7},{7,6},{8,9},{9,8},{10,11... | collective-permute-start | bytes 393224 | tf_op jit(solution)/shard_map/ppermute | solution.py:43

commit v4 on v3

--- a/solution.py
+++ b/solution.py
@@ -248,61 +248,45 @@
     return sum_up(arrived, part)
 
 
-def row_kernel(column_ref, out_ref, dout_ref, lse_ref, tail_ref, own_ref, other_ref):
-    step = pl.program_id(0)
-    heads = QUERY_HEADS // 2
+def row_kernel(column_ref, bitmap_ref, out_ref, dout_ref, lse_ref, segment_ref, own_ref, other_ref):
+    heads = MY_HEADS
     ones = jnp.ones((8, HEAD_SIZE), jnp.bfloat16)
-    rows = []
-    for i in range(heads):
-        cols = slice(i * HEAD_SIZE, (i + 1) * HEAD_SIZE)
-        product = out_ref[:, cols].astype(jnp.float32) * dout_ref[:, cols].astype(jnp.float32)
-        high = product.astype(jnp.bfloat16)
-        low = (product - high.astype(jnp.float32)).astype(jnp.bfloat16)
-        rows.append((nt(ones, high) + nt(ones, low))[:1])
-    delta = jnp.concatenate(rows, axis=0)
-
-    def fill(ref):
-        ref[0:heads, :] = lse_ref[...] * (-LOG2E)
-        ref[heads : 2 * heads, :] = delta
-        ref[2 * heads : SMALL_ROWS, :] = tail_ref[...]
-
-    @pl.when(step == column_ref[0])
-    def _():
-        fill(own_ref)
-
-    @pl.when(step != column_ref[0])
-    def _():
-        fill(other_ref)
-
-
-def row_values(column, out, dout, lse, seg_code, bitmap):
-    tail = jnp.concatenate(
-        [
-            seg_code.astype(jnp.float32)[None, :],
-            jnp.broadcast_to(bitmap.astype(jnp.float32)[None, :], (1, TILE)),
-            jnp.zeros((SMALL_ROWS - 2 * MY_HEADS - 2, TILE), jnp.float32),
-        ],
-        axis=0,
-    )
-    wide = pl.BlockSpec((TILE, Q_COLS), lambda j, c: (0, j))
+    segment = segment_ref[...]
+    seg_code = jnp.where(segment & 1 == 1, (segment + 1) >> 1, 0).astype(jnp.float32)
+    words = jnp.full((1, TILE), bitmap_ref[0], jnp.int32).astype(jnp.float32)
+    empty = jnp.zeros((SMALL_ROWS - 2 * heads - 2, TILE), jnp.float32)
+    for side in range(2):
+        rows = []
+        for i in range(side * heads, (side + 1) * heads):
+            cols = slice(i * HEAD_SIZE, (i + 1) * HEAD_SIZE)
+            product = out_ref[:, cols].astype(jnp.float32) * dout_ref[:, cols].astype(jnp.float32)
+            high = product.astype(jnp.bfloat16)
+            low = (product - high.astype(jnp.float32)).astype(jnp.bfloat16)
+            rows.append((nt(ones, high) + nt(ones, low))[:1])
+        neg_lse = lse_ref[side * heads : (side + 1) * heads, :] * (-LOG2E)
+        filled = jnp.concatenate([neg_lse, *rows, seg_code, words, empty], axis=0)
+
+        @pl.when(column_ref[0] == side)
+        def _():
+            own_ref[...] = filled
+
+        @pl.when(column_ref[0] != side)
+        def _():
+            other_ref[...] = filled
+
+
+def row_values(column, out, dout, lse, segment, bitmap):
+    here = pl.BlockSpec(memory_space=pltpu.VMEM)
     return pl.pallas_call(
         row_kernel,
-        grid_spec=pltpu.PrefetchScalarGridSpec(
-            num_scalar_prefetch=1,
-            grid=(2,),
-            in_specs=[
-                wide,
-                wide,
-                pl.BlockSpec((MY_HEADS, TILE), lambda j, c: (j, 0)),
-                pl.BlockSpec((SMALL_ROWS - 2 * MY_HEADS, TILE), lambda j, c: (0, 0)),
-            ],
-            out_specs=[pl.BlockSpec((SMALL_ROWS, TILE), lambda j, c: (0, 0))] * 2,
-        ),
+        in_specs=[pl.BlockSpec(memory_space=pltpu.SMEM)] * 2 + [here] * 4,
+        out_specs=[here] * 2,
         out_shape=[jax.ShapeDtypeStruct((SMALL_ROWS, TILE), jnp.float32)] * 2,
+        compiler_params=pltpu.CompilerParams(vmem_limit_bytes=16 * 1024 * 1024),
         cost_estimate=pl.CostEstimate(
             flops=4 * 8 * TILE * QUERY_HEADS * HEAD_SIZE, bytes_accessed=2**21, transcendentals=0
         ),
-    )(column[None].astype(jnp.int32), out, dout, lse, tail)
+    )(column[None].astype(jnp.int32), bitmap, out, dout, lse, segment[None, :])
 
 
 def tie(first, second):
@@ -339,7 +323,7 @@
     sent_q = jnp.concatenate(
         [half(query, 1 - column, Q_COLS, 1), half(dout, 1 - column, Q_COLS, 1)], axis=0
     )
-    smalls = row_values(column, out, dout, lse, seg_code, bitmap)
+    smalls = row_values(column, out, dout, lse, segment, bitmap)
     sm_own = smalls[0]
     sm_par = swap(smalls[1])
     sent_q, sm_par = lax.optimization_barrier((sent_q, sm_par))

time: 196 us -> 197 us (level)
  local copies, waits for them, and re-layouts: 1.29 us -> 4.92 us
  Pallas kernels: 33.6 us -> 31.6 us
    unnamed x6 -> x12, local copies, waits for them, and re-layouts: 0.02 us -> 3.82 us
  transfers between devices with their start and end apart: 21 -> 21, of which waited for: 10 -> 10; matrix products, arithmetic and copies ran while one was open for 2% -> 1% of each run, Pallas kernels for 17% -> 16%
where the time goes in v4:
time: 197 us; the launch traced here: 196 us
  starting transfers between devices  106 us (54%)
  waiting for transfers between devices  46.7 us (24%)
  Pallas kernels  31.6 us (16%)
  other arithmetic  5.54 us (3%)
  local copies, waits for them, and re-layouts  4.92 us (2%)
    ppermute x16, starting transfers between devices, shift(): lax.ppermute(array, AXES, [(i, (i + by) % count) for i in range(count)])  92.5 us
    ppermute x16, waiting for transfers between devices, shift(): lax.ppermute(array, AXES, [(i, (i + by) % count) for i in range(count)])  38.9 us
    pallas_call x5, Pallas kernels, pair_grads(): pl.pallas_call(functools.partial(pair_kernel, offsets, first, last), in_s...  29.5 us
    ppermute x5, starting transfers between devices, swap(): return lax.ppermute(array, AXES, [(i, i ^ 1) for i in range(count)])  13.2 us
    ppermute x5, waiting for transfers between devices, swap(): return lax.ppermute(array, AXES, [(i, i ^ 1) for i in range(count)])  7.81 us
  transfers between devices with their start and end apart: 21, of which 10 were waited for; matrix products, arithmetic and copies ran while one was open for 1% of the time, Pallas kernels for 16%

profile of v4, /device:TPU:32, one launch (start us, length us, event | category | flops | bytes accessed | tf_op | source)
XLA Modules:
  0.0 196.2 jit_solution(6660021710646660850)
XLA Ops:
  3.0 3.4 %collective-permute-start.2 = (bf16[272,256]{1,0:T(8,128)(2,1)}, bf16[272,256]{1,0:T(8,128)(2,1)S(1)}, u32[]{:S(2)}, u32[]{:S(2)}) collective-permute-start(bf16[272,256]{1,0:T(8,128)(2,1)} %pad_maximum_fusion.4), channel_id=1, source_target_pairs={{0,1},{1,0},{2,3},{3,2},{4,5},{5,4},{6,7},{7,6},{8,9},{9,8},{10,11... | collective-permute-start | bytes 417800 | tf_op jit(solution)/shard_map/ppermute | solution.py:43
  12.2 2.5 %collective-permute-start = (f32[40,128]{1,0:T(8,128)S(1)}, f32[40,128]{1,0:T(8,128)S(1)}, u32[]{:S(2)}, u32[]{:S(2)}) collective-permute-start(f32[40,128]{1,0:T(8,128)S(1)} %get-tuple-element.49), channel_id=1, source_target_pairs={{0,1},{1,0},{2,3},{3,2},{4,5},{5,4},{6,7},{7,6},{8,9},{9,8},{10,11... | collective-permute-start | bytes 61448 | tf_op jit(solution)/shard_map/ppermute | solution.py:43
  20.4 3.8 %collective-permute-start.4 = (bf16[528,256]{1,0:T(8,128)(2,1)S(1)}, bf16[528,256]{1,0:T(8,128)(2,1)S(1)}, u32[]{:S(2)}, u32[]{:S(2)}) collective-permute-start(bf16[528,256]{1,0:T(8,128)(2,1)S(1)} %pad_maximum_fusion.2.refs_8_), channel_id=1, source_target_pairs={{0,2},{1,3},{2,4},{3,5},{4,6},{5,7},{6,8},{7,9},{8,10},{9,11},{10,... | collective-permute-start | bytes 811016 | tf_op jit(solution)/shard_map/ppermute | solution.py:38
  24.3 13.9 %collective-permute-start.3 = (bf16[528,256]{1,0:T(8,128)(2,1)S(1)}, bf16[528,256]{1,0:T(8,128)(2,1)S(1)}, u32[]{:S(2)}, u32[]{:S(2)}) collective-permute-start(bf16[528,256]{1,0:T(8,128)(2,1)S(1)} %pad_maximum_fusion.2.refs_8_), channel_id=1, source_target_pairs={{0,16},{1,17},{2,18},{3,19},{4,20},{5,21},{6,22},{7,23},{8,24},{9,... | collective-permute-start | bytes 811016 | tf_op jit(solution)/shard_map/ppermute | solution.py:38
  38.2 2.9 %collective-permute-start.6 = (bf16[528,256]{1,0:T(8,128)(2,1)S(1)}, bf16[528,256]{1,0:T(8,128)(2,1)S(1)}, u32[]{:S(2)}, u32[]{:S(2)}) collective-permute-start(bf16[528,256]{1,0:T(8,128)(2,1)S(1)} %collective-permute-done.4.refs_9_), channel_id=1, source_target_pairs={{0,2},{1,3},{2,4},{3,5},{4,6},{5,7},{6,8},{7,9},{8,10},{9,11},{10,... | collective-permute-start | bytes 811016 | tf_op jit(solution)/shard_map/ppermute | solution.py:38
  44.2 7.6 %shard_map.105 = (bf16[512,256]{1,0:T(8,128)(2,1)S(1)}, bf16[512,256]{1,0:T(8,128)(2,1)S(1)}, f32[16,256,128]{2,1,0:T(8,128)S(1)}) custom-call(s32[2]{0:T(128)S(1)} %pad_add_fusion.where_ref, bf16[128,4096]{1,0:T(8,128)(2,1)S(1)} %copy-done.2, bf16[256,2048]{1,0:T(8,128)(2,1)S(1)} %collective-permute-done.1.q_par.refs_1_, bf16[128,4096]{1,0:T(8,128)(2,1)S(1)} %copy-done.1, ...), custom_call_target="tpu_custom_call" | custom-call | flops 2684354560 | bytes 8388608 | tf_op jit(solution)/shard_map/pallas_call | solution.py:225
  52.6 14.1 %collective-permute-start.5 = (bf16[528,256]{1,0:T(8,128)(2,1)S(1)}, bf16[528,256]{1,0:T(8,128)(2,1)S(1)}, u32[]{:S(2)}, u32[]{:S(2)}) collective-permute-start(bf16[528,256]{1,0:T(8,128)(2,1)S(1)} %collective-permute-done.3), channel_id=1, source_target_pairs={{0,510},{1,511},{2,0},{3,1},{4,2},{5,3},{6,4},{7,5},{8,6},{9,7},{1... | collective-permute-start | bytes 811016 | tf_op jit(solution)/shard_map/ppermute | solution.py:38
  66.8 3.2 %collective-permute-start.8 = (bf16[528,256]{1,0:T(8,128)(2,1)S(1)}, bf16[528,256]{1,0:T(8,128)(2,1)S(1)}, u32[]{:S(2)}, u32[]{:S(2)}) collective-permute-start(bf16[528,256]{1,0:T(8,128)(2,1)S(1)} %collective-permute-done.6.refs_9_), channel_id=1, source_target_pairs={{0,2},{1,3},{2,4},{3,5},{4,6},{5,7},{6,8},{7,9},{8,10},{9,11},{10,... | collective-permute-start | bytes 811016 | tf_op jit(solution)/shard_map/ppermute | solution.py:38
  70.0 5.6 %shard_map.106 = (bf16[256,256]{1,0:T(8,128)(2,1)S(1)}, bf16[512,256]{1,0:T(8,128)(2,1)S(1)}, f32[16,256,128]{2,1,0:T(8,128)S(1)}) custom-call(s32[2]{0:T(128)S(1)} %pad_add_fusion.where_ref, bf16[128,4096]{1,0:T(8,128)(2,1)S(1)} %copy-done.2, bf16[256,2048]{1,0:T(8,128)(2,1)S(1)} %collective-permute-done.1.q_par.refs_1_, ...), custom_call_target="tpu_custom_call", output_to_operand_aliasing={{2}: (11, {})} | custom-call | flops 2013265920 | bytes 8388608 | tf_op jit(solution)/shard_map/pallas_call | solution.py:225
  75.6 6.3 %collective-permute-start.7 = (bf16[528,256]{1,0:T(8,128)(2,1)S(1)}, bf16[528,256]{1,0:T(8,128)(2,1)S(1)}, u32[]{:S(2)}, u32[]{:S(2)}) collective-permute-start(bf16[528,256]{1,0:T(8,128)(2,1)S(1)} %collective-permute-done.5.refs_8_), channel_id=1, source_target_pairs={{0,510},{1,511},{2,0},{3,1},{4,2},{5,3},{6,4},{7,5},{8,6},{9,7},{1... | collective-permute-start | bytes 811016 | tf_op jit(solution)/shard_map/ppermute | solution.py:38
  83.9 6.0 %shard_map.107 = (bf16[512,256]{1,0:T(8,128)(2,1)S(1)}, bf16[512,256]{1,0:T(8,128)(2,1)S(1)}, f32[16,256,128]{2,1,0:T(8,128)S(1)}) custom-call(s32[2]{0:T(128)S(1)} %pad_add_fusion.where_ref, bf16[128,4096]{1,0:T(8,128)(2,1)S(1)} %copy-done.2, bf16[256,2048]{1,0:T(8,128)(2,1)S(1)} %collective-permute-done.1.q_par.refs_1_, ...), custom_call_target="tpu_custom_call", output_to_operand_aliasing={{2}: (11, {})} | custom-call | flops 2684354560 | bytes 8388608 | tf_op jit(solution)/shard_map/pallas_call | solution.py:225
  89.9 5.8 %collective-permute-done.10.refs_9_ = bf16[528,256]{1,0:T(8,128)(2,1)S(1)} collective-permute-done((bf16[528,256]{1,0:T(8,128)(2,1)S(1)}, bf16[528,256]{1,0:T(8,128)(2,1)S(1)}, u32[]{:S(2)}, u32[]{:S(2)}) %collective-permute-start.10) | collective-permute-done | bytes 270368 | tf_op jit(solution)/shard_map/ppermute | solution.py:38
  95.8 9.2 %collective-permute-start.9 = (bf16[528,256]{1,0:T(8,128)(2,1)S(1)}, bf16[528,256]{1,0:T(8,128)(2,1)S(1)}, u32[]{:S(2)}, u32[]{:S(2)}) collective-permute-start(bf16[528,256]{1,0:T(8,128)(2,1)S(1)} %collective-permute-done.7.refs_8_), channel_id=1, source_target_pairs={{0,510},{1,511},{2,0},{3,1},{4,2},{5,3},{6,4},{7,5},{8,6},{9,7},{1... | collective-permute-start | bytes 811016 | tf_op jit(solution)/shard_map/ppermute | solution.py:38
  105.0 6.0 %shard_map.108 = (bf16[512,256]{1,0:T(8,128)(2,1)S(1)}, bf16[512,256]{1,0:T(8,128)(2,1)S(1)}, f32[16,256,128]{2,1,0:T(8,128)S(1)}) custom-call(s32[2]{0:T(128)S(1)} %pad_add_fusion.where_ref, bf16[128,4096]{1,0:T(8,128)(2,1)S(1)} %copy-done.2, bf16[256,2048]{1,0:T(8,128)(2,1)S(1)} %collective-permute-done.1.q_par.refs_1_, ...), custom_call_target="tpu_custom_call", output_to_operand_aliasing={{2}: (11, {})} | custom-call | flops 2684354560 | bytes 8388608 | tf_op jit(solution)/shard_map/pallas_call | solution.py:225
  111.0 3.8 %collective-permute-start.11 = (bf16[512,256]{1,0:T(8,128)(2,1)S(1)}, bf16[512,256]{1,0:T(8,128)(2,1)S(1)}, u32[]{:S(2)}, u32[]{:S(2)}) collective-permute-start(bf16[512,256]{1,0:T(8,128)(2,1)S(1)} %get-tuple-element.79), channel_id=1, source_target_pairs={{0,510},{1,511},{2,0},{3,1},{4,2},{5,3},{6,4},{7,5},{8,6},{9,7},{1... | collective-permute-start | bytes 786440 | tf_op jit(solution)/shard_map/ppermute | solution.py:38
  114.9 4.3 %shard_map.109 = (bf16[512,256]{1,0:T(8,128)(2,1)S(1)}, bf16[128,2048]{1,0:T(8,128)(2,1)S(1)}, bf16[128,2048]{1,0:T(8,128)(2,1)S(1)}) custom-call(s32[2]{0:T(128)S(1)} %pad_add_fusion.where_ref, bf16[128,4096]{1,0:T(8,128)(2,1)S(1)} %copy-done.2, bf16[256,2048]{1,0:T(8,128)(2,1)S(1)} %collective-permute-done.1.q_par.refs_1_, ...), custom_call_target="tpu_custom_call" | custom-call | flops 1342177280 | bytes 8388608 | tf_op jit(solution)/shard_map/pallas_call | solution.py:225
  121.3 3.8 %collective-permute-start.16 = (bf16[512,256]{1,0:T(8,128)(2,1)S(1)}, bf16[512,256]{1,0:T(8,128)(2,1)S(1)}, u32[]{:S(2)}, u32[]{:S(2)}) collective-permute-start(bf16[512,256]{1,0:T(8,128)(2,1)S(1)} %add_convert_fusion.4), channel_id=1, source_target_pairs={{0,510},{1,511},{2,0},{3,1},{4,2},{5,3},{6,4},{7,5},{8,6},{9,7},{1... | collective-permute-start | bytes 786440 | tf_op jit(solution)/shard_map/ppermute | solution.py:38
  129.9 6.7 %collective-permute-start.17 = (bf16[512,256]{1,0:T(8,128)(2,1)S(1)}, bf16[512,256]{1,0:T(8,128)(2,1)S(1)}, u32[]{:S(2)}, u32[]{:S(2)}) collective-permute-start(bf16[512,256]{1,0:T(8,128)(2,1)S(1)} %add_convert_fusion.3), channel_id=1, source_target_pairs={{0,510},{1,511},{2,0},{3,1},{4,2},{5,3},{6,4},{7,5},{8,6},{9,7},{1... | collective-permute-start | bytes 786440 | tf_op jit(solution)/shard_map/ppermute | solution.py:38
  140.9 2.7 %collective-permute-start.12 = (bf16[128,2048]{1,0:T(8,128)(2,1)S(1)}, bf16[128,2048]{1,0:T(8,128)(2,1)S(1)}, u32[]{:S(2)}, u32[]{:S(2)}) collective-permute-start(bf16[128,2048]{1,0:T(8,128)(2,1)S(1)} %get-tuple-element.81), channel_id=1, source_target_pairs={{0,1},{1,0},{2,3},{3,2},{4,5},{5,4},{6,7},{7,6},{8,9},{9,8},{10,11... | collective-permute-start | bytes 1572872 | tf_op jit(solution)/shard_map/ppermute | solution.py:43
  143.6 12.6 %collective-permute-done.15 = bf16[512,256]{1,0:T(8,128)(2,1)S(1)} collective-permute-done((bf16[512,256]{1,0:T(8,128)(2,1)S(1)}, bf16[512,256]{1,0:T(8,128)(2,1)S(1)}, u32[]{:S(2)}, u32[]{:S(2)}) %collective-permute-start.15) | collective-permute-done | bytes 262176 | tf_op jit(solution)/shard_map/ppermute | solution.py:38
  156.3 14.5 %collective-permute-start.18 = (bf16[512,256]{1,0:T(8,128)(2,1)S(1)}, bf16[512,256]{1,0:T(8,128)(2,1)S(1)}, u32[]{:S(2)}, u32[]{:S(2)}) collective-permute-start(bf16[512,256]{1,0:T(8,128)(2,1)S(1)} %add_convert_fusion.2), channel_id=1, source_target_pairs={{0,510},{1,511},{2,0},{3,1},{4,2},{5,3},{6,4},{7,5},{8,6},{9,7},{1... | collective-permute-start | bytes 786440 | tf_op jit(solution)/shard_map/ppermute | solution.py:38
  172.9 3.0 %collective-permute-done.18 = bf16[512,256]{1,0:T(8,128)(2,1)S(1)} collective-permute-done((bf16[512,256]{1,0:T(8,128)(2,1)S(1)}, bf16[512,256]{1,0:T(8,128)(2,1)S(1)}, u32[]{:S(2)}, u32[]{:S(2)}) %collective-permute-start.18) | collective-permute-done | bytes 262176 | tf_op jit(solution)/shard_map/ppermute | solution.py:38
  175.8 12.0 %collective-permute-done.19 = bf16[512,256]{1,0:T(8,128)(2,1)S(1)} collective-permute-done((bf16[512,256]{1,0:T(8,128)(2,1)S(1)}, bf16[512,256]{1,0:T(8,128)(2,1)S(1)}, u32[]{:S(2)}, u32[]{:S(2)}) %collective-permute-start.19) | collective-permute-done | bytes 262176 | tf_op jit(solution)/shard_map/ppermute | solution.py:38
  191.3 3.6 %collective-permute-done.20 = bf16[256,256]{1,0:T(8,128)(2,1)S(1)} collective-permute-done((bf16[256,256]{1,0:T(8,128)(2,1)S(1)}, bf16[256,256]{1,0:T(8,128)(2,1)S(1)}, u32[]{:S(2)}, u32[]{:S(2)}) %collective-permute-start.20) | collective-permute-done | bytes 131104 | tf_op jit(solution)/shard_map/ppermute | solution.py:43
  (66 shorter events, 37.0 us)
Async XLA Ops:
  3.0 17.3 %collective-permute-start.2 = (bf16[272,256]{1,0:T(8,128)(2,1)}, bf16[272,256]{1,0:T(8,128)(2,1)S(1)}, u32[]{:S(2)}, u32[]{:S(2)}) collective-permute-start(bf16[272,256]{1,0:T(8,128)(2,1)} %pad_maximum_fusion.4), channel_id=1, source_target_pairs={{0,1},{1,0},{2,3},{3,2},{4,5},{5,4},{6,7},{7,6},{8,9},{9,8},{10,11... | collective-permute-start | bytes 417800 | tf_op jit(solution)/shard_map/ppermute | solution.py:43
  7.0 1.2 copy-start
  10.9 3.8 %copy-start.1 = (bf16[128,4096]{1,0:T(8,128)(2,1)S(1)}, bf16[128,4096]{1,0:T(8,128)(2,1)}, u32[]{:S(2)}) copy-start(bf16[128,4096]{1,0:T(8,128)(2,1)} %refs_2_.9) | copy-start | bytes 3145732
  10.9 3.8 %copy-start.2 = (bf16[128,4096]{1,0:T(8,128)(2,1)S(1)}, bf16[128,4096]{1,0:T(8,128)(2,1)}, u32[]{:S(2)}) copy-start(bf16[128,4096]{1,0:T(8,128)(2,1)} %refs_0_.9) | copy-start | bytes 3145732
  12.2 5.7 %collective-permute-start = (f32[40,128]{1,0:T(8,128)S(1)}, f32[40,128]{1,0:T(8,128)S(1)}, u32[]{:S(2)}, u32[]{:S(2)}) collective-permute-start(f32[40,128]{1,0:T(8,128)S(1)} %get-tuple-element.49), channel_id=1, source_target_pairs={{0,1},{1,0},{2,3},{3,2},{4,5},{5,4},{6,7},{7,6},{8,9},{9,8},{10,11... | collective-permute-start | bytes 61448 | tf_op jit(solution)/shard_map/ppermute | solution.py:43
  17.9 25.6 %collective-permute-start.1 = (bf16[256,2048]{1,0:T(8,128)(2,1)}, bf16[256,2048]{1,0:T(8,128)(2,1)S(1)}, u32[]{:S(2)}, u32[]{:S(2)}) collective-permute-start(bf16[256,2048]{1,0:T(8,128)(2,1)} %pad_maximum_fusion), channel_id=1, source_target_pairs={{0,1},{1,0},{2,3},{3,2},{4,5},{5,4},{6,7},{7,6},{8,9},{9,8},{10,11... | collective-permute-start | bytes 3145736 | tf_op jit(solution)/shard_map/ppermute | solution.py:43
  20.4 17.8 %collective-permute-start.4 = (bf16[528,256]{1,0:T(8,128)(2,1)S(1)}, bf16[528,256]{1,0:T(8,128)(2,1)S(1)}, u32[]{:S(2)}, u32[]{:S(2)}) collective-permute-start(bf16[528,256]{1,0:T(8,128)(2,1)S(1)} %pad_maximum_fusion.2.refs_8_), channel_id=1, source_target_pairs={{0,2},{1,3},{2,4},{3,5},{4,6},{5,7},{6,8},{7,9},{8,10},{9,11},{10,... | collective-permute-start | bytes 811016 | tf_op jit(solution)/shard_map/ppermute | solution.py:38
  24.3 28.3 %collective-permute-start.3 = (bf16[528,256]{1,0:T(8,128)(2,1)S(1)}, bf16[528,256]{1,0:T(8,128)(2,1)S(1)}, u32[]{:S(2)}, u32[]{:S(2)}) collective-permute-start(bf16[528,256]{1,0:T(8,128)(2,1)S(1)} %pad_maximum_fusion.2.refs_8_), channel_id=1, source_target_pairs={{0,16},{1,17},{2,18},{3,19},{4,20},{5,21},{6,22},{7,23},{8,24},{9,... | collective-permute-start | bytes 811016 | tf_op jit(solution)/shard_map/ppermute | solution.py:38
  38.2 28.5 %collective-permute-start.6 = (bf16[528,256]{1,0:T(8,128)(2,1)S(1)}, bf16[528,256]{1,0:T(8,128)(2,1)S(1)}, u32[]{:S(2)}, u32[]{:S(2)}) collective-permute-start(bf16[528,256]{1,0:T(8,128)(2,1)S(1)} %collective-permute-done.4.refs_9_), channel_id=1, source_target_pairs={{0,2},{1,3},{2,4},{3,5},{4,6},{5,7},{6,8},{7,9},{8,10},{9,11},{10,... | collective-permute-start | bytes 811016 | tf_op jit(solution)/shard_map/ppermute | solution.py:38
  52.6 23.0 %collective-permute-start.5 = (bf16[528,256]{1,0:T(8,128)(2,1)S(1)}, bf16[528,256]{1,0:T(8,128)(2,1)S(1)}, u32[]{:S(2)}, u32[]{:S(2)}) collective-permute-start(bf16[528,256]{1,0:T(8,128)(2,1)S(1)} %collective-permute-done.3), channel_id=1, source_target_pairs={{0,510},{1,511},{2,0},{3,1},{4,2},{5,3},{6,4},{7,5},{8,6},{9,7},{1... | collective-permute-start | bytes 811016 | tf_op jit(solution)/shard_map/ppermute | solution.py:38
  66.8 15.2 %collective-permute-start.8 = (bf16[528,256]{1,0:T(8,128)(2,1)S(1)}, bf16[528,256]{1,0:T(8,128)(2,1)S(1)}, u32[]{:S(2)}, u32[]{:S(2)}) collective-permute-start(bf16[528,256]{1,0:T(8,128)(2,1)S(1)} %collective-permute-done.6.refs_9_), channel_id=1, source_target_pairs={{0,2},{1,3},{2,4},{3,5},{4,6},{5,7},{6,8},{7,9},{8,10},{9,11},{10,... | collective-permute-start | bytes 811016 | tf_op jit(solution)/shard_map/ppermute | solution.py:38
  75.6 14.3 %collective-permute-start.7 = (bf16[528,256]{1,0:T(8,128)(2,1)S(1)}, bf16[528,256]{1,0:T(8,128)(2,1)S(1)}, u32[]{:S(2)}, u32[]{:S(2)}) collective-permute-start(bf16[528,256]{1,0:T(8,128)(2,1)S(1)} %collective-permute-done.5.refs_8_), channel_id=1, source_target_pairs={{0,510},{1,511},{2,0},{3,1},{4,2},{5,3},{6,4},{7,5},{8,6},{9,7},{1... | collective-permute-start | bytes 811016 | tf_op jit(solution)/shard_map/ppermute | solution.py:38
  82.0 13.8 %collective-permute-start.10 = (bf16[528,256]{1,0:T(8,128)(2,1)S(1)}, bf16[528,256]{1,0:T(8,128)(2,1)S(1)}, u32[]{:S(2)}, u32[]{:S(2)}) collective-permute-start(bf16[528,256]{1,0:T(8,128)(2,1)S(1)} %collective-permute-done.8.refs_9_), channel_id=1, source_target_pairs={{0,2},{1,3},{2,4},{3,5},{4,6},{5,7},{6,8},{7,9},{8,10},{9,11},{10,... | collective-permute-start | bytes 811016 | tf_op jit(solution)/shard_map/ppermute | solution.py:38
  95.8 19.1 %collective-permute-start.9 = (bf16[528,256]{1,0:T(8,128)(2,1)S(1)}, bf16[528,256]{1,0:T(8,128)(2,1)S(1)}, u32[]{:S(2)}, u32[]{:S(2)}) collective-permute-start(bf16[528,256]{1,0:T(8,128)(2,1)S(1)} %collective-permute-done.7.refs_8_), channel_id=1, source_target_pairs={{0,510},{1,511},{2,0},{3,1},{4,2},{5,3},{6,4},{7,5},{8,6},{9,7},{1... | collective-permute-start | bytes 811016 | tf_op jit(solution)/shard_map/ppermute | solution.py:38
  111.0 10.2 %collective-permute-start.11 = (bf16[512,256]{1,0:T(8,128)(2,1)S(1)}, bf16[512,256]{1,0:T(8,128)(2,1)S(1)}, u32[]{:S(2)}, u32[]{:S(2)}) collective-permute-start(bf16[512,256]{1,0:T(8,128)(2,1)S(1)} %get-tuple-element.79), channel_id=1, source_target_pairs={{0,510},{1,511},{2,0},{3,1},{4,2},{5,3},{6,4},{7,5},{8,6},{9,7},{1... | collective-permute-start | bytes 786440 | tf_op jit(solution)/shard_map/ppermute | solution.py:38
  119.2 8.3 %collective-permute-start.13 = (bf16[512,256]{1,0:T(8,128)(2,1)S(1)}, bf16[512,256]{1,0:T(8,128)(2,1)S(1)}, u32[]{:S(2)}, u32[]{:S(2)}) collective-permute-start(bf16[512,256]{1,0:T(8,128)(2,1)S(1)} %get-tuple-element.82), channel_id=1, source_target_pairs={{0,2},{1,3},{2,4},{3,5},{4,6},{5,7},{6,8},{7,9},{8,10},{9,11},{10,... | collective-permute-start | bytes 786440 | tf_op jit(solution)/shard_map/ppermute | solution.py:38
  121.3 8.5 %collective-permute-start.16 = (bf16[512,256]{1,0:T(8,128)(2,1)S(1)}, bf16[512,256]{1,0:T(8,128)(2,1)S(1)}, u32[]{:S(2)}, u32[]{:S(2)}) collective-permute-start(bf16[512,256]{1,0:T(8,128)(2,1)S(1)} %add_convert_fusion.4), channel_id=1, source_target_pairs={{0,510},{1,511},{2,0},{3,1},{4,2},{5,3},{6,4},{7,5},{8,6},{9,7},{1... | collective-permute-start | bytes 786440 | tf_op jit(solution)/shard_map/ppermute | solution.py:38
  127.5 11.4 %collective-permute-start.14 = (bf16[512,256]{1,0:T(8,128)(2,1)S(1)}, bf16[512,256]{1,0:T(8,128)(2,1)S(1)}, u32[]{:S(2)}, u32[]{:S(2)}) collective-permute-start(bf16[512,256]{1,0:T(8,128)(2,1)S(1)} %add_convert_fusion.6), channel_id=1, source_target_pairs={{0,2},{1,3},{2,4},{3,5},{4,6},{5,7},{6,8},{7,9},{8,10},{9,11},{10,... | collective-permute-start | bytes 786440 | tf_op jit(solution)/shard_map/ppermute | solution.py:38
  129.9 13.7 %collective-permute-start.17 = (bf16[512,256]{1,0:T(8,128)(2,1)S(1)}, bf16[512,256]{1,0:T(8,128)(2,1)S(1)}, u32[]{:S(2)}, u32[]{:S(2)}) collective-permute-start(bf16[512,256]{1,0:T(8,128)(2,1)S(1)} %add_convert_fusion.3), channel_id=1, source_target_pairs={{0,510},{1,511},{2,0},{3,1},{4,2},{5,3},{6,4},{7,5},{8,6},{9,7},{1... | collective-permute-start | bytes 786440 | tf_op jit(solution)/shard_map/ppermute | solution.py:38
  139.0 17.2 %collective-permute-start.15 = (bf16[512,256]{1,0:T(8,128)(2,1)S(1)}, bf16[512,256]{1,0:T(8,128)(2,1)S(1)}, u32[]{:S(2)}, u32[]{:S(2)}) collective-permute-start(bf16[512,256]{1,0:T(8,128)(2,1)S(1)} %add_convert_fusion.5), channel_id=1, source_target_pairs={{0,2},{1,3},{2,4},{3,5},{4,6},{5,7},{6,8},{7,9},{8,10},{9,11},{10,... | collective-permute-start | bytes 786440 | tf_op jit(solution)/shard_map/ppermute | solution.py:38
  140.9 31.9 %collective-permute-start.12 = (bf16[128,2048]{1,0:T(8,128)(2,1)S(1)}, bf16[128,2048]{1,0:T(8,128)(2,1)S(1)}, u32[]{:S(2)}, u32[]{:S(2)}) collective-permute-start(bf16[128,2048]{1,0:T(8,128)(2,1)S(1)} %get-tuple-element.81), channel_id=1, source_target_pairs={{0,1},{1,0},{2,3},{3,2},{4,5},{5,4},{6,7},{7,6},{8,9},{9,8},{10,11... | collective-permute-start | bytes 1572872 | tf_op jit(solution)/shard_map/ppermute | solution.py:43
  156.3 19.5 %collective-permute-start.18 = (bf16[512,256]{1,0:T(8,128)(2,1)S(1)}, bf16[512,256]{1,0:T(8,128)(2,1)S(1)}, u32[]{:S(2)}, u32[]{:S(2)}) collective-permute-start(bf16[512,256]{1,0:T(8,128)(2,1)S(1)} %add_convert_fusion.2), channel_id=1, source_target_pairs={{0,510},{1,511},{2,0},{3,1},{4,2},{5,3},{6,4},{7,5},{8,6},{9,7},{1... | collective-permute-start | bytes 786440 | tf_op jit(solution)/shard_map/ppermute | solution.py:38
  170.9 17.0 %collective-permute-start.19 = (bf16[512,256]{1,0:T(8,128)(2,1)S(1)}, bf16[512,256]{1,0:T(8,128)(2,1)S(1)}, u32[]{:S(2)}, u32[]{:S(2)}) collective-permute-start(bf16[512,256]{1,0:T(8,128)(2,1)S(1)} %add_convert_fusion.1), channel_id=1, source_target_pairs={{0,496},{1,497},{2,498},{3,499},{4,500},{5,501},{6,502},{7,503},{8... | collective-permute-start | bytes 786440 | tf_op jit(solution)/shard_map/ppermute | solution.py:38
  188.0 6.9 %collective-permute-start.20 = (bf16[256,256]{1,0:T(8,128)(2,1)S(1)}, bf16[256,256]{1,0:T(8,128)(2,1)S(1)}, u32[]{:S(2)}, u32[]{:S(2)}) collective-permute-start(bf16[256,256]{1,0:T(8,128)(2,1)S(1)} %broadcast_select_fusion.5), channel_id=1, source_target_pairs={{0,1},{1,0},{2,3},{3,2},{4,5},{5,4},{6,7},{7,6},{8,9},{9,8},{10,11... | collective-permute-start | bytes 393224 | tf_op jit(solution)/shard_map/ppermute | solution.py:43
  (3 other events, 2.6 us)
